TPU v7x, 32 devices: a whole 2x2x4 slice. The times are simulated.
32 devices in a mesh: vis: 8 (over z, x), head: 4 (over y, core).
Axes of the slice: x: 2, y: 2, z: 4, core: 2. Of those that a mesh axis runs over, the one named last changes fastest.
Arguments:
- patches: bfloat16 [3072, 1280], P('vis'), may hold values from -6 to 6
- norm_gain: float32 [1280], replicated, may hold values from 0.4 to 1.6
- w_qkv: bfloat16 [1280, 3, 1280], P(None, None, 'head'), may hold values from -1 to 1
- w_out: bfloat16 [1280, 1280], P(None, 'head'), may hold values from -0.15625 to 0.15625
- grad_y: bfloat16 [3072, 1280], P('vis'), may hold values from -6 to 6
- window_ids: int32 [3072], replicated, may hold values from 0 to 63, never falling along the last dimension, each value on 1 to 64 neighbouring positions
Outputs:
- grad_x: bfloat16 [3072, 1280], P('vis', 'head')
- grad_qkv: float32 [1280, 3, 1280], P('vis', None, 'head')
- grad_out: float32 [1280, 1280], P('vis', 'head')
- grad_gain: float32 [1280], P('head')
Inputs may be any that keep to these rules, and one draw needn't show every extreme that they name: `window_ids`: window numbers never fall along the patches, and each window holds 1 to 64 patches, one exactly 64.
All inputs are finite; a program needn't handle non-finite values.
Results may differ from a plain program's by a relative error of at most 0.03.
Values may be sent and summed in bfloat16 or wider, within the bound.
No kernel may reach another device: no remote copies, remote signals or barrier semaphores. Data moves between devices by JAX's collectives and lax.ppermute only.
A program may use at most 64 MiB of HBM per device.

v0:
```python
import jax
import jax.numpy as jnp
from jax import lax
from jax.sharding import PartitionSpec as P

HEAD_DIM = 80
WIN = 64


norm_epsilon = 1e-06


def extended_2(block, sides, width):
    for axis, dim in sides:
        count = lax.axis_size(axis)
        forward = [(i, i + 1) for i in range(count - 1)]
        backward = [(target, source) for source, target in forward]
        low = lax.ppermute(
            lax.slice_in_dim(block, block.shape[dim] - width, None, axis=dim), axis, forward
        )
        high = lax.ppermute(lax.slice_in_dim(block, 0, width, axis=dim), axis, backward)
        block = jnp.concatenate([low, block, high], axis=dim)
    return block


def from_behind(block, axis, distance):
    devices = range(lax.axis_size(axis))
    route = [(i - distance, i) for i in devices if i - distance in devices]
    return lax.ppermute(block, axis, route)


def attention_grads(query, keyval, own_ids, key_ids, grad_att):
    f32 = jnp.float32
    row_count = query.shape[0]
    key_span = keyval.shape[0]
    heads = query.shape[1] // HEAD_DIM
    scale = HEAD_DIM ** (-0.5)
    q_heads = query.reshape(row_count, heads, HEAD_DIM)
    k_heads = keyval[:, 0].reshape(key_span, heads, HEAD_DIM)
    v_heads = keyval[:, 1].reshape(key_span, heads, HEAD_DIM)
    g_heads = grad_att.reshape(row_count, heads, HEAD_DIM)
    scores = jnp.einsum("rhe,khe->hrk", q_heads, k_heads, preferred_element_type=f32) * scale
    same_window = own_ids[:, None] == key_ids[None, :]
    scores = jnp.where(same_window[None], scores, -1e30)
    highest = jnp.max(scores, axis=2, keepdims=True)
    weights = jnp.exp(scores - highest)
    weights = weights / jnp.sum(weights, axis=2, keepdims=True)
    probs = weights.astype(jnp.bfloat16)
    attended = jnp.einsum("hrk,khe->rhe", probs, v_heads, preferred_element_type=f32).astype(
        jnp.bfloat16
    )
    delta = jnp.sum(attended.astype(f32) * g_heads.astype(f32), axis=2)
    dprob = jnp.einsum("rhe,khe->hrk", g_heads, v_heads, preferred_element_type=f32)
    dscore = (weights * (dprob - jnp.transpose(delta)[:, :, None]) * scale).astype(jnp.bfloat16)
    grad_q = jnp.einsum("hrk,khe->rhe", dscore, k_heads, preferred_element_type=f32).astype(
        jnp.bfloat16
    )
    grad_k = jnp.einsum("hrk,rhe->khe", dscore, q_heads, preferred_element_type=f32)
    grad_v = jnp.einsum("hrk,rhe->khe", probs, g_heads, preferred_element_type=f32)
    key_grads = jnp.stack([grad_k.reshape(key_span, -1), grad_v.reshape(key_span, -1)], axis=1)
    return (attended.reshape(row_count, -1), grad_q.reshape(row_count, -1), key_grads)


def per_device(patches, norm_gain, w_qkv, w_out, grad_y, window_ids):
    f32 = jnp.float32
    bf16 = jnp.bfloat16
    row_count, feature_count = patches.shape
    vis_index = lax.axis_index("vis")
    head_index = lax.axis_index("head")
    share_width = feature_count // lax.axis_size("head")
    inputs = patches.astype(f32)
    inverse = lax.rsqrt(jnp.mean(inputs * inputs, axis=1, keepdims=True) + norm_epsilon)
    normed = (inputs * inverse * norm_gain[None, :]).astype(bf16)
    project = jnp.einsum("rd,dcj->rcj", normed, w_qkv, preferred_element_type=f32).astype(bf16)
    keyval = project[:, 1:]
    extended = extended_2(keyval, (("vis", 0),), WIN)
    padded_ids = jnp.pad(window_ids, (WIN, WIN), constant_values=-1)
    first_row = vis_index * row_count
    own_ids = lax.dynamic_slice_in_dim(window_ids, first_row, row_count, 0)
    key_ids = lax.dynamic_slice_in_dim(padded_ids, first_row, row_count + 2 * WIN, 0)
    grad_att = jnp.dot(grad_y, w_out, preferred_element_type=f32).astype(bf16)
    attended, grad_q, key_grads = attention_grads(
        project[:, 0], extended, own_ids, key_ids, grad_att
    )
    center = key_grads[WIN : WIN + row_count]
    from_below = from_behind(key_grads[:WIN].astype(jnp.bfloat16), "vis", -1).astype(jnp.float32)
    from_above = from_behind(key_grads[WIN + row_count :].astype(jnp.bfloat16), "vis", 1).astype(
        jnp.float32
    )
    center = center.at[row_count - WIN :].add(from_below)
    center = center.at[:WIN].add(from_above)
    grad_proj = jnp.concatenate([grad_q[:, None, :], center.astype(bf16)], axis=1)
    partial_normed = jnp.einsum("rcj,dcj->rd", grad_proj, w_qkv, preferred_element_type=f32)
    share_start = head_index * share_width
    grad_normed = lax.psum(partial_normed.astype(jnp.bfloat16), "head").astype(jnp.float32)
    scaled = grad_normed * norm_gain[None, :]
    product_mean = jnp.mean(scaled * inputs, axis=1, keepdims=True)
    full_x = grad_y.astype(f32) + inverse * (scaled - inputs * inverse * inverse * product_mean)
    grad_x = lax.dynamic_slice_in_dim(full_x, share_start, share_width, 1).astype(bf16)
    gain_full = jnp.sum(grad_normed * inputs * inverse, axis=0)
    gain_part = lax.dynamic_slice_in_dim(gain_full, share_start, share_width, 0)
    grad_gain = lax.psum(gain_part, "vis")
    qkv_local = jnp.einsum("rd,rcj->dcj", normed, grad_proj, preferred_element_type=f32)
    out_local = jnp.einsum("ro,ri->oi", grad_y, attended, preferred_element_type=f32)
    grad_qkv, grad_out = (
        lax.psum_scatter(qkv_local, "vis", scatter_dimension=0, tiled=True),
        lax.psum_scatter(out_local, "vis", scatter_dimension=0, tiled=True),
    )
    return (grad_x, grad_qkv, grad_out, grad_gain)


def solution(mesh):
    in_specs = (P("vis", None), P(), P(None, None, "head"), P(None, "head"), P("vis", None), P())
    out_specs = (P("vis", "head"), P("vis", None, "head"), P("vis", "head"), P("head"))
    return jax.shard_map(
        per_device, mesh=mesh, in_specs=in_specs, out_specs=out_specs, check_vma=False
    )
```

profile of v0, /device:TPU:0, one launch (start us, length us, event | category | flops | bytes accessed | tf_op | source)
XLA Modules:
  0.0 260.7 jit_solution(2182086812770170848)
XLA Ops:
  8.0 0.0 copy-start
  8.0 0.0 all-reduce.3.cloned.1.call-start
  8.1 1.6 fusion.3
  9.7 0.3 copy-done
  10.0 2.8 %convolution_convert_fusion = bf16[384,3,320]{0,2,1:T(8,128)(2,1)S(1)} fusion(bf16[1280,3,320]{0,2,1:T(8,128)(2,1)S(1)} %copy-done, f32[1280]{0:T(1024)} %param.11, bf16[384,1280]{1,0:T(8,128)(2,1)} %param.10, f32[384]{0:T(512)S(1)} %add_rsqrt_fusion), kind=kOutput, calls=%fused_computation.27 | convolution fusion | flops 946053120 | bytes 4184576 | tf_op jit(solution)/shard_map/rd,dcj->rcj/dot_general | solution.py:74
  12.8 0.0 copy-done.9
  12.9 0.0 copy-start.6
  12.9 0.9 copy-done.6
  13.7 0.8 fusion.29
  14.5 5.5 %collective-permute-start = (bf16[64,2,320]{0,2,1:T(8,128)(2,1)}, bf16[64,2,320]{0,2,1:T(8,128)(2,1)}, u32[]{:S(2)}, u32[]{:S(2)}) collective-permute-start(bf16[64,2,320]{0,2,1:T(8,128)(2,1)} %get-tuple-element.40), channel_id=1, source_target_pairs={{0,4},{4,8},{8,12},{12,16},{16,20},{20,24},{24,28},{1,5},{5,9},{9,... | collective-permute-start | bytes 245768 | tf_op jit(solution)/shard_map/ppermute | solution.py:18
  20.0 1.3 collective-permute-start.1
  21.3 0.0 copy-start.7
  21.3 0.1 pad_dynamic-slice_fusion
  21.4 0.1 dynamic_slice.12
  21.5 2.5 convolution_convert_fusion.3
  24.0 0.2 broadcast_compare_fusion
  24.2 0.1 slice.92
  24.3 0.0 collective-permute-done
  24.3 3.6 %collective-permute-done.1 = bf16[64,2,320]{0,2,1:T(8,128)(2,1)} collective-permute-done((bf16[64,2,320]{0,2,1:T(8,128)(2,1)}, bf16[64,2,320]{0,2,1:T(8,128)(2,1)}, u32[]{:S(2)}, u32[]{:S(2)}) %collective-permute-start.1) | collective-permute-done | bytes 81952 | tf_op jit(solution)/shard_map/ppermute | solution.py:21
  27.9 1.3 pad_maximum_fusion.2
  29.2 3.5 %fusion.32 = (f32[4,384]{1,0:T(4,128)}, f32[4,384,512]{2,1,0:T(8,128)}) fusion(pred[384,512]{1,0:T(8,128)(4,1)S(1)} %broadcast_compare_fusion, bf16[384,4,80]{0,2,1:T(8,128)(2,1)S(1)} %bitcast.62, bf16[512,4,80]{0,2,1:T(8,128)(2,1)S(1)} %bitcast.58), kind=kOutput, calls=%fused_computation.60 | convolution fusion | flops 128975360 | bytes 3921920 | tf_op jit(solution)/shard_map/sub | solution.py:46
  32.8 2.2 fusion.11
  35.0 0.0 copy-start.13
  35.0 0.4 fusion.34
  35.4 1.3 multiply_reduce_fusion
  36.8 0.2 copy-done.3
  36.9 1.0 multiply_convert_fusion
  37.9 1.3 convolution_convert_fusion.1
  39.2 0.4 fusion.33
  39.6 0.1 fusion.10
  39.7 0.8 fusion.30
  40.5 4.4 %collective-permute-start.3 = (bf16[64,2,320]{0,2,1:T(8,128)(2,1)}, bf16[64,2,320]{0,2,1:T(8,128)(2,1)}, u32[]{:S(2)}, u32[]{:S(2)}) collective-permute-start(bf16[64,2,320]{0,2,1:T(8,128)(2,1)} %get-tuple-element.42), channel_id=1, source_target_pairs={{0,4},{4,8},{8,12},{12,16},{16,20},{20,24},{24,28},{1,5},{5,9},{9,... | collective-permute-start | bytes 245768 | tf_op jit(solution)/shard_map/ppermute | solution.py:29
  44.9 1.3 collective-permute-start.2
  46.2 0.3 fusion.12
  46.5 5.6 %collective-permute-done.2 = bf16[64,2,320]{0,2,1:T(8,128)(2,1)S(1)} collective-permute-done((bf16[64,2,320]{0,2,1:T(8,128)(2,1)S(1)}, bf16[64,2,320]{0,2,1:T(8,128)(2,1)S(1)}, u32[]{:S(2)}, u32[]{:S(2)}) %collective-permute-start.2) | collective-permute-done | bytes 81952 | tf_op jit(solution)/shard_map/ppermute | solution.py:29
  52.1 0.8 fusion.20
  52.8 2.2 scatter-add.6
  55.0 0.0 collective-permute-done.3
  55.1 1.7 slice_add_fusion
  56.7 1.9 scatter-add.9
  58.6 0.1 convert_element_type.74
  58.7 0.0 copy-start.2
  58.7 0.8 copy-done.2
  59.5 3.3 %fusion.1 = bf16[384,1280]{1,0:T(8,128)(2,1)} fusion(bf16[1280,3,320]{0,2,1:T(8,128)(2,1)S(1)} %copy-done, bf16[384,2,320]{0,2,1:T(8,128)(2,1)S(1)} %convert_element_type.74, bf16[384,1,320]{0,2,1:T(8,128)(2,1)} %bitcast.56), kind=kOutput, calls=%fused_computation.10 | convolution fusion | flops 944578560 | bytes 4177920 | tf_op jit(solution)/shard_map/rcj,dcj->rd/dot_general | solution.py:93
  62.7 0.0 all-reduce.3.cloned.1.call-update
  62.8 0.0 reduce-scatter.7.cloned.1.call-start
  62.8 0.0 copy-done.5
  62.8 2.7 %convolution_bitcast_fusion.1 = f32[1280,320]{0,1:T(8,128)} fusion(bf16[384,320]{0,1:T(8,128)(2,1)} %bitcast.67, bf16[384,1280]{1,0:T(8,128)(2,1)S(1)} %copy-done.5), kind=kOutput, calls=%fused_computation.9 | convolution fusion | flops 314572800 | bytes 2867200 | tf_op jit(solution)/shard_map/ro,ri->oi/dot_general | solution.py:104
  65.5 2.9 %copy.18 = f32[1280,320]{1,0:T(8,128)} copy(f32[1280,320]{0,1:T(8,128)} %convolution_bitcast_fusion.1) | data formatting | bytes 3276800
  68.4 0.0 reduce-scatter.7.cloned.1.call-update
  68.4 0.2 reduce-scatter.5.cloned.1.call-start
  68.7 0.0 copy-done.1
  68.7 0.0 copy-done.10
  68.7 0.0 copy-done.11
  68.7 5.5 %fusion.18 = f32[1280,3,320]{2,0,1:T(8,128)} fusion(bf16[384,2,320]{0,2,1:T(8,128)(2,1)} %copy-done.2, bf16[384,1,320]{0,2,1:T(8,128)(2,1)} %bitcast.57, f32[1280]{0:T(1024)S(1)} %copy-done.11, bf16[384,1280]{1,0:T(8,128)(2,1)S(1)} %copy-done.1, f32[384]{0:T(512)S(1)} %copy-done.10), kind=kOutput, calls=%fused_computation.44 | convolution fusion | flops 947159040 | bytes 6642176 | tf_op jit(solution)/shard_map/rd,rcj->dcj/dot_general | solution.py:103
  74.2 0.0 reduce-scatter.5.cloned.1.call-update
  74.2 26.6 %all-reduce.3.cloned.1.call-done = bf16[384,1280]{1,0:T(8,128)(2,1)} async-done(((bf16[384,1280]{1,0:T(8,128)(2,1)}), bf16[384,1280]{1,0:T(8,128)(2,1)}) %all-reduce.3.cloned.1.call-update) | async-done | bytes 983056 | tf_op jit(solution)/shard_map/psum | solution.py:95
  100.8 1.9 fusion.6
  102.7 0.1 dynamic_slice.15
  102.8 1.6 fusion.16
  104.4 0.9 copy.14
  105.3 22.0 %psum.15 = f32[320]{0:T(512)} all-reduce(f32[320]{0:T(512)S(1)} %dynamic_slice.15), channel_id=1, replica_groups=mesh['vis'=8,'head'=4] {'vis'}, use_global_device_ids=true, to_apply=%region_9.10 | all-reduce | flops 320 | bytes 2560 | tf_op jit(solution)/shard_map/psum | solution.py:102
  127.2 10.7 %reduce-scatter.7.cloned.1.call-done = f32[160,320]{1,0:T(8,128)} async-done(((f32[1280,320]{1,0:T(8,128)}), f32[160,320]{1,0:T(8,128)}) %reduce-scatter.7.cloned.1.call-update) | async-done | bytes 204816
  138.0 115.3 %reduce-scatter.5.cloned.1.call-done = f32[160,3,320]{2,0,1:T(8,128)} async-done(((f32[1280,3,320]{2,0,1:T(8,128)}), f32[160,3,320]{2,0,1:T(8,128)}) %reduce-scatter.5.cloned.1.call-update) | async-done | bytes 614416 | tf_op jit(solution)/shard_map/reduce_scatter | solution.py:106
  (18 shorter events, 0.1 us)
Async XLA Ops:
  8.0 2.0 copy-start
  8.0 92.8 %all-reduce.3.cloned.1.call-start = ((), (), s32[]{:S(2)}) async-start(), calls=%async_computation.2 | async-start | bytes 1966080 | tf_op jit(solution)/shard_map/psum | solution.py:95
  10.0 2.9 %copy-start.9 = (f32[384]{0:T(512)}, f32[384]{0:T(512)S(1)}, u32[]{:S(2)}) copy-start(f32[384]{0:T(512)S(1)} %add_rsqrt_fusion) | copy-start | bytes 4612
  10.0 11.3 %copy-start.12 = (s32[3072]{0:T(1024)S(1)}, s32[3072]{0:T(1024)}, u32[]{:S(2)}) copy-start(s32[3072]{0:T(1024)} %param.15) | copy-start | bytes 36868
  10.0 11.5 %copy-start.4 = (bf16[384,1280]{1,0:T(8,128)(2,1)S(1)}, bf16[384,1280]{1,0:T(8,128)(2,1)}, u32[]{:S(2)}) copy-start(bf16[384,1280]{1,0:T(8,128)(2,1)} %param.14) | copy-start | bytes 2949124
  12.9 0.9 copy-start.6
  14.5 9.8 %collective-permute-start = (bf16[64,2,320]{0,2,1:T(8,128)(2,1)}, bf16[64,2,320]{0,2,1:T(8,128)(2,1)}, u32[]{:S(2)}, u32[]{:S(2)}) collective-permute-start(bf16[64,2,320]{0,2,1:T(8,128)(2,1)} %get-tuple-element.40), channel_id=1, source_target_pairs={{0,4},{4,8},{8,12},{12,16},{16,20},{20,24},{24,28},{1,5},{5,9},{9,... | collective-permute-start | bytes 245768 | tf_op jit(solution)/shard_map/ppermute | solution.py:18
  20.0 7.9 %collective-permute-start.1 = (bf16[64,2,320]{0,2,1:T(8,128)(2,1)}, bf16[64,2,320]{0,2,1:T(8,128)(2,1)}, u32[]{:S(2)}, u32[]{:S(2)}) collective-permute-start(bf16[64,2,320]{0,2,1:T(8,128)(2,1)} %get-tuple-element.41), channel_id=1, source_target_pairs={{4,0},{8,4},{12,8},{16,12},{20,16},{24,20},{28,24},{5,1},{9,5},{13... | collective-permute-start | bytes 245768 | tf_op jit(solution)/shard_map/ppermute | solution.py:21
  21.3 2.9 %copy-start.7 = (bf16[384,3,320]{0,2,1:T(8,128)(2,1)S(1)}, bf16[384,3,320]{0,2,1:T(8,128)(2,1)}, u32[]{:S(2)}) copy-start(bf16[384,3,320]{0,2,1:T(8,128)(2,1)} %copy-done.6) | copy-start | bytes 2211844
  32.8 2.2 copy-start.8
  35.0 1.9 copy-start.3
  35.0 1.9 copy-start.13
  40.5 14.6 %collective-permute-start.3 = (bf16[64,2,320]{0,2,1:T(8,128)(2,1)}, bf16[64,2,320]{0,2,1:T(8,128)(2,1)}, u32[]{:S(2)}, u32[]{:S(2)}) collective-permute-start(bf16[64,2,320]{0,2,1:T(8,128)(2,1)} %get-tuple-element.42), channel_id=1, source_target_pairs={{0,4},{4,8},{8,12},{12,16},{16,20},{20,24},{24,28},{1,5},{5,9},{9,... | collective-permute-start | bytes 245768 | tf_op jit(solution)/shard_map/ppermute | solution.py:29
  44.9 7.2 %collective-permute-start.2 = (bf16[64,2,320]{0,2,1:T(8,128)(2,1)S(1)}, bf16[64,2,320]{0,2,1:T(8,128)(2,1)S(1)}, u32[]{:S(2)}, u32[]{:S(2)}) collective-permute-start(bf16[64,2,320]{0,2,1:T(8,128)(2,1)S(1)} %get-tuple-element.43), channel_id=1, source_target_pairs={{4,0},{8,4},{12,8},{16,12},{20,16},{24,20},{28,24},{5,1},{9,5},{13... | collective-permute-start | bytes 245768 | tf_op jit(solution)/shard_map/ppermute | solution.py:29
  58.7 0.8 copy-start.2
  59.5 3.4 %copy-start.5 = (bf16[384,1280]{1,0:T(8,128)(2,1)S(1)}, bf16[384,1280]{1,0:T(8,128)(2,1)}, u32[]{:S(2)}) copy-start(bf16[384,1280]{1,0:T(8,128)(2,1)} %param.14) | copy-start | bytes 2949124
  62.8 75.2 %reduce-scatter.7.cloned.1.call-start = ((), (), s32[]{:S(2)}) async-start(), calls=%async_computation.4 | async-start | bytes 2211840
  65.5 3.1 %copy-start.1 = (bf16[384,1280]{1,0:T(8,128)(2,1)S(1)}, bf16[384,1280]{1,0:T(8,128)(2,1)}, u32[]{:S(2)}) copy-start(bf16[384,1280]{1,0:T(8,128)(2,1)} %param.10) | copy-start | bytes 2949124
  65.5 3.1 %copy-start.10 = (f32[384]{0:T(512)S(1)}, f32[384]{0:T(512)}, u32[]{:S(2)}) copy-start(f32[384]{0:T(512)} %copy-done.9) | copy-start | bytes 4612
  65.5 3.1 %copy-start.11 = (f32[1280]{0:T(1024)S(1)}, f32[1280]{0:T(1024)}, u32[]{:S(2)}) copy-start(f32[1280]{0:T(1024)} %param.11) | copy-start | bytes 15364
  68.4 184.9 %reduce-scatter.5.cloned.1.call-start = ((), (), s32[]{:S(2)}) async-start(), calls=%async_computation.3 | async-start | bytes 6635520 | tf_op jit(solution)/shard_map/reduce_scatter | solution.py:106
Sparse Core Ops, SparseCore 0:
  62.9 37.8 all-reduce.2
Sparse Core Ops, SparseCore 1:
  68.5 69.4 reduce-scatter.6
  142.1 111.2 reduce-scatter.4
where the time goes:
time: 261 us
  waiting for transfers between devices  162 us (62%)
  matrix products  24.7 us (9%)
  blocking collectives  22 us (8%)
  between operations  15.8 us (6%)
  starting transfers between devices  12.8 us (5%)
  local copies, waits for them, and re-layouts  11.8 us (5%)
  other arithmetic  11.8 us (5%)
    reduce_scatter x1, waiting for transfers between devices, per_device(): lax.psum_scatter(qkv_local, 'vis', scatter_dimension=0, tiled=True)  115 us
    psum x1, waiting for transfers between devices, per_device(): lax.psum(partial_normed.astype(jnp.bfloat16), 'head').astype(jnp.float32)  26.6 us
    psum x1, blocking collectives, per_device(): grad_gain = lax.psum(gain_part, 'vis')  22 us
    unnamed x4, waiting for transfers between devices  10.8 us
    unnamed x30, local copies, waits for them, and re-layouts  5.85 us
    ppermute x2, starting transfers between devices, from_behind(): return lax.ppermute(block, axis, route)  5.69 us
    ppermute x2, waiting for transfers between devices, from_behind(): return lax.ppermute(block, axis, route)  5.6 us
    dot_general x1, matrix products, per_device(): jnp.einsum('rd,rcj->dcj', normed, grad_proj, preferred_element_type=f32)  5.52 us
  transfers between devices with their start and end apart: 7, of which 5 were waited for; matrix products, arithmetic and copies ran while one was open for 8% of the time, Pallas kernels for 0%

commit v1 on v0

v1 whole, which is shorter than its diff:
```python
import functools

import jax
import jax.numpy as jnp
from jax import lax
from jax.experimental import pallas as pl
from jax.experimental.pallas import tpu as pltpu
from jax.sharding import PartitionSpec as P

HEAD_DIM = 80
WIN = 64
TILE = 128
EPSILON = 1e-06
F32 = jnp.float32
BF16 = jnp.bfloat16
VMEM_LIMIT = 24 << 20
WEIGHT = 300

NN = (((1,), (0,)), ((), ()))
NT = (((1,), (1,)), ((), ()))
TN = (((0,), (0,)), ((), ()))


def dot(a, b, dims=NN):
    return lax.dot_general(a, b, dims, preferred_element_type=F32)


ANY = pl.BlockSpec(memory_space=pl.ANY)


def call(kernel, outs, *args, weight=WEIGHT, after=(), own_copies=(), **kwargs):
    size = lambda t: t.size * t.dtype.itemsize
    moved = sum(size(a) for a in args) + sum(size(o) for o in outs)
    whole = pl.BlockSpec(memory_space=pltpu.VMEM)
    hbm = pl.BlockSpec(memory_space=pltpu.HBM)
    specs = [hbm if i in own_copies else whole for i in range(len(args))] + [ANY] * len(after)
    if after:
        body, first = kernel, len(args)
        kernel = lambda *refs: body(*refs[:first], *refs[first + len(after) :])
    args = args + tuple(after)
    return pl.pallas_call(
        kernel,
        in_specs=specs,
        out_shape=outs,
        compiler_params=pltpu.CompilerParams(vmem_limit_bytes=VMEM_LIMIT),
        cost_estimate=pl.CostEstimate(
            flops=weight * 10 * moved, bytes_accessed=weight * moved, transcendentals=0
        ),
        **kwargs,
    )(*args)


def shape(dims, dtype=BF16):
    return jax.ShapeDtypeStruct(dims, dtype)


def turned_row(row, count):
    tile = jnp.transpose(jnp.broadcast_to(row, (TILE, TILE)))
    return jnp.concatenate([tile] * count, axis=1)


def rows_to_columns(ref, out_ref):
    rows, features = ref.shape
    squares = jnp.zeros((8, rows), F32)
    for t in range(features // TILE):
        x = jnp.transpose(ref[:, t * TILE : (t + 1) * TILE])
        out_ref[t * TILE : (t + 1) * TILE, :] = x
        x = x.astype(F32)
        squares = squares + jnp.sum((x * x).reshape(TILE // 8, 8, rows), axis=0)
    return jnp.sum(squares, axis=0, keepdims=True)


def normalise(x_t_ref, inverse, gain_ref, normed_ref, gain_columns=None):
    features, rows = x_t_ref.shape
    for t in range(features // TILE):
        gain = turned_row(gain_ref[t : t + 1, :], rows // TILE)
        normed_ref[span(t), :] = (x_t_ref[span(t), :].astype(F32) * inverse * gain).astype(BF16)
        if gain_columns is not None:
            gain_columns[span(t), :] = gain[:, :TILE]


def span(t):
    return slice(t * TILE, (t + 1) * TILE)


def head_band(h):
    return slice(h * HEAD_DIM, (h + 1) * HEAD_DIM)


def half_shifted(before, after):
    lane = lax.broadcasted_iota(jnp.int32, after.shape, 1)
    return jnp.where(lane < TILE // 2, pltpu.roll(before, TILE // 2, 1), pltpu.roll(after, TILE // 2, 1))


def window_rows(ids_ref, tiles):
    vis, count = lax.axis_index("vis"), lax.axis_size("vis")
    own = tiles - 1
    first = vis * own
    id_row = lambda t: ids_ref[pl.ds(t, 1), :]
    before = jnp.where(vis > 0, id_row(jnp.maximum(first - 1, 0)), -1)
    after = jnp.where(vis < count - 1, id_row(jnp.minimum(first + own, count * own - 1)), -2)
    line = [before] + [id_row(first + t) for t in range(own)] + [after]
    ids = [half_shifted(line[t], line[t + 1]) for t in range(tiles)]
    counts = [row != after[:, :1] for row in ids]
    upper = lax.broadcasted_iota(jnp.int32, (1, TILE), 1) >= TILE // 2
    counts[0] = upper | ((ids[0] == line[1][:, :1]) & (ids[0] >= 0))
    counts[-1] = counts[-1] & ~upper
    return [row.astype(F32) for row in ids], counts


def attention(blocks, heads, ids, q_at, g_at, wide_at, tall_at):
    scale = HEAD_DIM ** (-0.5)
    columns = {t: turned_row(ids[t], 1) for near in blocks.values() for t in near}
    attended, grad_q, grad_k, grad_v = {}, {}, {}, {}
    for b, near in blocks.items():
        bias = [jnp.where(columns[t] == ids[b], 0.0, -1e30) for t in near]
        bias = jnp.concatenate(bias, axis=0)
        wide = lambda c, h: jnp.concatenate([wide_at(c, h, t) for t in near], axis=1)
        tall = lambda c, h: jnp.concatenate([tall_at(c, h, t) for t in near], axis=0)
        q = [q_at(h, b) for h in heads]
        g = [g_at(h, b) for h in heads]
        scores = [dot(tall(0, h), q[h]) for h in heads]
        dprob = [dot(tall(1, h), g[h]) for h in heads]
        weights = []
        for h in heads:
            s = scores[h] * scale + bias
            e = jnp.exp(s - jnp.max(s, axis=0, keepdims=True))
            weights.append(e * (1.0 / jnp.sum(e, axis=0, keepdims=True)))
        probs = [w.astype(BF16) for w in weights]
        attended[b] = [dot(wide(1, h), probs[h]).astype(BF16) for h in heads]
        dscore = []
        for h in heads:
            delta = jnp.sum(attended[b][h].astype(F32) * g[h].astype(F32), axis=0, keepdims=True)
            dscore.append((weights[h] * (dprob[h] - delta) * scale).astype(BF16))
        grad_q[b] = [dot(wide(0, h), dscore[h]).astype(BF16) for h in heads]
        gk = [dot(q[h], dscore[h], NT) for h in heads]
        gv = [dot(g[h], probs[h], NT) for h in heads]
        for i, t in enumerate(near):
            for sums, part in ((grad_k, gk), (grad_v, gv)):
                part = [p[:, span(i)] for p in part]
                sums[t] = [x + y for x, y in zip(sums[t], part)] if t in sums else part
    return attended, grad_q, grad_k, grad_v


def only(rows, value):
    return jnp.where(rows, value, jnp.zeros_like(value))


def own_kernel(
    x_any, gain_any, w_any, gy_any, wo_any, ids_ref,
    normed_ref, gy_t_ref, inverse_ref, x_own_ref, gy_own_ref, gain_own_ref, first_rows_ref,
    kv_ref, attended_ref, gq_ref, gkv_ref, w_ref, wo_ref,
    x_ref, gain_ref, gy_ref, x_t, gain_columns, q_ref, ga_ref, turned, sems,
):
    places, features = x_ref.shape
    share = wo_ref.shape[0]
    tiles = places // TILE
    rows = places - TILE
    own = pl.ds(WIN, rows)
    copies = [
        pltpu.make_async_copy(x_any, x_ref.at[own], sems.at[0]),
        pltpu.make_async_copy(gain_any, gain_ref, sems.at[1]),
        pltpu.make_async_copy(w_any, w_ref, sems.at[2]),
        pltpu.make_async_copy(gy_any, gy_ref.at[own], sems.at[3]),
        pltpu.make_async_copy(wo_any, wo_ref, sems.at[4]),
    ]
    for copy in copies:
        copy.start()
    empty = jnp.zeros((WIN, features), BF16)
    for ref in (x_ref, gy_ref):
        ref[:WIN, :] = empty
        ref[WIN + rows :, :] = empty
    copies[0].wait()
    inverse = lax.rsqrt(rows_to_columns(x_ref, x_t) / features + EPSILON)
    inverse_ref[...] = jnp.broadcast_to(inverse, inverse_ref.shape)
    copies[1].wait()
    normalise(x_t, inverse, gain_ref, normed_ref, gain_columns)
    copies[2].wait()
    q_ref[...] = dot(w_ref[0], normed_ref[...]).astype(BF16)
    for c in range(2):
        kv_ref[c] = dot(w_ref[1 + c], normed_ref[...]).astype(BF16)
    copies[3].wait()
    for t in range(features // TILE):
        gy_t_ref[span(t), :] = jnp.transpose(gy_ref[:, span(t)])
    copies[4].wait()
    ga_ref[...] = dot(wo_ref[...], gy_t_ref[...]).astype(BF16)
    at = pl.ds(pl.multiple_of(lax.axis_index("head") * share, share), share)
    x_own_ref[...] = x_t[at, :]
    gy_own_ref[...] = gy_t_ref[at, :]
    gain_own_ref[...] = gain_columns[at, :]
    first_rows_ref[:WIN, :] = x_ref[WIN : 2 * WIN, :]
    first_rows_ref[WIN:, :] = gy_ref[WIN : 2 * WIN, :]

    heads = range(share // HEAD_DIM)
    for c in range(2):
        for h in heads:
            turned[c, h] = jnp.transpose(kv_ref[c, head_band(h), :])
    ids, counts = window_rows(ids_ref, tiles)
    blocks = {b: [t for t in (b - 1, b, b + 1) if t < tiles] for b in range(1, tiles)}
    attended, grad_q, grad_k, grad_v = attention(
        blocks, heads, ids,
        lambda h, b: q_ref[head_band(h), span(b)], lambda h, b: ga_ref[head_band(h), span(b)],
        lambda c, h, t: kv_ref[c, head_band(h), span(t)], lambda c, h, t: turned[c, h, span(t), :],
    )
    for h in heads:
        for t in range(tiles):
            if t in blocks:
                attended_ref[head_band(h), span(t)] = only(counts[t], attended[t][h])
                gq_ref[head_band(h), span(t)] = only(counts[t], grad_q[t][h])
            gkv_ref[0, head_band(h), span(t)] = only(counts[t], grad_k[t][h])
            gkv_ref[1, head_band(h), span(t)] = only(counts[t], grad_v[t][h])
    attended_ref[:, :TILE] = jnp.zeros((share, TILE), BF16)
    gq_ref[:, :TILE] = jnp.zeros((share, TILE), BF16)


def halo_kernel(
    edge_ref, first_rows_ref, gain_ref, w_ref, wo_ref, ids_ref, kv_ref, attended_in, gq_in, gkv_in,
    inverse_in, x_own_in, gy_own_in,
    attended_ref, gq_ref, gkv_ref, normed_ref, gy_t_ref, inverse_ref, x_own_ref, gy_own_ref,
    both, x_t, near_keys, turned,
):
    features, share = edge_ref.shape[1], wo_ref.shape[0]
    tiles = attended_ref.shape[1] // TILE
    for i in range(2):
        both[i, :WIN, :] = edge_ref[i * WIN : (i + 1) * WIN, :]
        both[i, WIN:, :] = first_rows_ref[i * WIN : (i + 1) * WIN, :]
    inverse = lax.rsqrt(rows_to_columns(both.at[0], x_t) / features + EPSILON)
    normalise(x_t, inverse, gain_ref, normed_ref)
    for t in range(features // TILE):
        gy_t_ref[span(t), :] = jnp.transpose(both[1, :, span(t)])
    q = dot(w_ref[0], normed_ref[...]).astype(BF16)
    g = dot(wo_ref[...], gy_t_ref[...]).astype(BF16)
    heads = range(share // HEAD_DIM)
    for c in range(2):
        near_keys[c, :, :TILE] = dot(w_ref[1 + c], normed_ref[...]).astype(BF16)
        near_keys[c, :, TILE:] = kv_ref[c, :, span(1)]
        for h in heads:
            turned[c, h] = jnp.transpose(near_keys[c, head_band(h), :])
    ids, counts = window_rows(ids_ref, tiles)
    attended, grad_q, grad_k, grad_v = attention(
        {0: [0, 1]}, heads, ids, lambda h, b: q[head_band(h)], lambda h, b: g[head_band(h)],
        lambda c, h, t: near_keys[c, head_band(h), span(t)], lambda c, h, t: turned[c, h, span(t), :],
    )
    rest = slice(TILE, tiles * TILE)
    at = pl.ds(pl.multiple_of(lax.axis_index("head") * share, share), share)
    for out, old, value in (
        (inverse_ref, inverse_in, jnp.broadcast_to(inverse, (8, TILE))),
        (x_own_ref, x_own_in, x_t[at, :]),
        (gy_own_ref, gy_own_in, gy_t_ref[at, :]),
    ):
        out[:, :TILE] = value
        out[:, rest] = old[:, rest]
    attended_ref[:, rest] = attended_in[:, rest]
    gq_ref[:, rest] = gq_in[:, rest]
    for c, sums in ((0, grad_k), (1, grad_v)):
        gkv_ref[c, :, 2 * TILE :] = gkv_in[c, :, 2 * TILE :].astype(BF16)
        for h in heads:
            for t in (0, 1):
                total = gkv_in[c, head_band(h), span(t)] + only(counts[t], sums[t][h])
                gkv_ref[c, head_band(h), span(t)] = total.astype(BF16)
    for h in heads:
        attended_ref[head_band(h), :TILE] = only(counts[0], attended[0][h])
        gq_ref[head_band(h), :TILE] = only(counts[0], grad_q[0][h])


def halo_rows_kernel(x_any, gy_any, out_ref, sems):
    last = pl.ds(x_any.shape[0] - WIN, WIN)
    copies = [
        pltpu.make_async_copy(x_any.at[last], out_ref.at[pl.ds(0, WIN)], sems.at[0]),
        pltpu.make_async_copy(gy_any.at[last], out_ref.at[pl.ds(WIN, WIN)], sems.at[1]),
    ]
    for copy in copies:
        copy.start()
    for copy in copies:
        copy.wait()


def places(left, bit):
    step = 1 << (len(left) - 1 - left.index(bit))
    return [p for p in range(1 << len(left)) if not p & step], step


def side_blocks(left, bit):
    base, step = places(left, bit)
    mine = (lax.axis_index("vis") >> bit) & 1
    return [[p + step * which for p in base] for which in (1 - mine, mine)]


def gathered(own_ref, halo_ref, scratch, part, left, bits):
    sub = part // len(bits)
    to = 0
    for chain, bit in enumerate(bits):
        for side in side_blocks(left, bit):
            for p in side:
                at = pl.ds(pl.multiple_of(p * part + chain * sub, 16), sub)
                scratch[to : to + sub, :TILE] = halo_ref[at, :]
                scratch[to : to + sub, TILE:] = own_ref[at, TILE:]
                to += sub


def out_query_product_kernel(part, left, bits, a_ref, a_halo_ref, b_ref, c_ref, c_halo_ref, d_ref, *refs):
    outs, (a_rows, c_rows) = refs[:-2], refs[-2:]
    share, rows = b_ref.shape
    gathered(a_ref, a_halo_ref, a_rows, part, left, bits)
    gathered(c_ref, c_halo_ref, c_rows, part, left, bits)
    gap = jnp.zeros((-share % TILE, rows), BF16)
    b = jnp.transpose(jnp.concatenate([b_ref[...], gap], axis=0))
    d = jnp.transpose(jnp.concatenate([gap, d_ref[...]], axis=0))
    shared = b.shape[1] - TILE
    count = outs[0].shape[0]
    for i, out in enumerate(outs):
        at = slice(i * count, (i + 1) * count)
        one, two = dot(a_rows[at, :], b), dot(c_rows[at, :], d)
        out[:, :shared] = one[:, :shared].astype(out.dtype)
        out[:, shared : shared + TILE] = (one[:, shared:] + two[:, :TILE]).astype(out.dtype)
        out[:, shared + TILE :] = two[:, TILE:].astype(out.dtype)


def pair_product_kernel(part, left, bits, a_ref, a_halo_ref, b_ref, *refs):
    outs, a_rows = refs[:-1], refs[-1]
    share, rows = b_ref.shape[1:]
    gathered(a_ref, a_halo_ref, a_rows, part, left, bits)
    b = jnp.transpose(b_ref[...].reshape(2 * share, rows))
    count = outs[0].shape[0]
    for i, out in enumerate(outs):
        out[...] = dot(a_rows[i * count : (i + 1) * count, :], b).astype(out.dtype)


def add_kernel(sub, lefts, bits, *refs):
    chains = len(bits)
    ins, outs = refs[: 2 * chains], refs[2 * chains :]
    joined = len(outs) < 2 * chains
    for chain, (left, bit) in enumerate(zip(lefts, bits)):
        keep_ref, came_ref = ins[2 * chain : 2 * chain + 2]
        first = chain if joined else 0
        for side, out in zip(side_blocks(left, bit), outs if joined else outs[2 * chain : 2 * chain + 2]):
            for i, p in enumerate(side):
                at = pl.ds(pl.multiple_of(p * sub, 16), sub)
                total = keep_ref[at, :] + came_ref[at, :].astype(F32)
                out[(first + i) * sub : (first + i + 1) * sub, :] = total.astype(out.dtype)


def split_whole(total, sub, left, bit):
    rows = lambda p: lax.dynamic_slice_in_dim(total, p * sub, sub, 0)
    send, keep = [jnp.concatenate([rows(p) for p in side], axis=0) for side in side_blocks(left, bit)]
    return [send.astype(BF16), keep]


def split_product(product, part, left, bits):
    sub = part // len(bits)
    by_chain = product.reshape(-1, len(bits), sub, product.shape[1])
    out = []
    for chain, bit in enumerate(bits):
        out += split_whole(by_chain[:, chain].reshape(-1, product.shape[1]), sub, left, bit)
    return out


def halves(rows, width, chains):
    return [shape((rows // 2, width)), shape((rows // 2, width), F32)] * chains


def out_query_product(part, left, bits, a, a_halo, b, c, c_halo, d):
    features = a.shape[0]
    share, rows = b.shape
    if part % (16 * len(bits)):
        a = jnp.concatenate([a_halo, a[:, TILE:]], axis=1)
        c = jnp.concatenate([c_halo, c[:, TILE:]], axis=1)
        product = jnp.concatenate([dot(a, b, NT), dot(c, d, NT)], axis=1)
        return split_product(product, part, left, bits)
    return call(
        functools.partial(out_query_product_kernel, part, left, bits),
        halves(features // len(bits), 2 * share, len(bits)), a, a_halo, b, c, c_halo, d,
        scratch_shapes=[pltpu.VMEM((features, rows), BF16)] * 2,
    )


def pair_product(part, left, bits, a, a_halo, b, after):
    features = a.shape[0]
    _, share, rows = b.shape
    if part % (16 * len(bits)):
        a = jnp.concatenate([a_halo, a[:, TILE:]], axis=1)
        return split_product(dot(a, b.reshape(2 * share, rows), NT), part, left, bits)
    return call(
        functools.partial(pair_product_kernel, part, left, bits),
        halves(features // len(bits), 2 * share, len(bits)), a, a_halo, b, after=after,
        scratch_shapes=[pltpu.VMEM((features, rows), BF16)],
    )


def add_split(sub, lefts, bits, pairs, after, weight):
    joined = len(lefts[0]) == 1 and len(set(bits)) == 1
    if sub % 16:
        parts = sum(
            [split_whole(k + c.astype(F32), sub, l, b) for (k, c), l, b in zip(pairs, lefts, bits)], []
        )
        return [jnp.concatenate(parts[i::2], axis=0) for i in range(2)] if joined else parts
    outs = halves(*pairs[0][0].shape, len(bits))
    if joined:
        outs = [shape((len(bits) * sub, o.shape[1]), o.dtype) for o in outs[:2]]
    return call(
        functools.partial(add_kernel, sub, lefts, bits), outs, *[t for pair in pairs for t in pair],
        after=after, weight=weight,
    )


def finish_out_query_kernel(*refs):
    ins, (out_ref, query_ref) = refs[:-2], refs[-2:]
    sub, width = ins[0].shape
    for chain in range(len(ins) // 2):
        total = ins[2 * chain][...] + ins[2 * chain + 1][...].astype(F32)
        rows = slice(chain * sub, (chain + 1) * sub)
        out_ref[rows, :] = total[:, : width // 2]
        query_ref[rows, :] = total[:, width // 2 :]


def finish_kernel(query_ref, *refs):
    ins, qkv_ref = refs[:-1], refs[-1]
    sub, width = ins[0].shape
    qkv_ref[0] = query_ref[...]
    for chain in range(len(ins) // 2):
        total = ins[2 * chain][...] + ins[2 * chain + 1][...].astype(F32)
        rows = slice(chain * sub, (chain + 1) * sub)
        qkv_ref[1, rows, :] = total[:, : width // 2]
        qkv_ref[2, rows, :] = total[:, width // 2 :]


def normed_grad_kernel(gq_ref, gkv_ref, w_ref, gain_ref, x_ref, halo_ref, send_ref, keep_ref):
    half, padded, rows = send_ref.shape
    share = padded - 16
    features = w_ref.shape[2]
    g = [jnp.transpose(gq_ref[...]), jnp.transpose(gkv_ref[0]), jnp.transpose(gkv_ref[1])]
    total = dot(g[0], w_ref[0]) + dot(g[1], w_ref[1]) + dot(g[2], w_ref[2])
    gap = jnp.zeros((TILE - WIN, features), BF16)
    x = jnp.concatenate([halo_ref[:WIN, :], x_ref[...], gap], axis=0)
    sums = jnp.zeros((rows, TILE), F32)
    for t in range(features // TILE):
        sums = sums + total[:, span(t)] * gain_ref[t : t + 1, :] * x[:, span(t)].astype(F32)
    row = jnp.broadcast_to(jnp.sum(jnp.transpose(sums), axis=0, keepdims=True), (16, rows))
    low = row - row.astype(BF16).astype(F32)
    extra = jnp.where(lax.broadcasted_iota(jnp.int32, row.shape, 0) < 8, row, low).astype(BF16)
    turned = jnp.transpose(total.astype(BF16))
    odd = (lax.axis_index("head") & 1) == 1
    for h in range(half):
        even_block = turned[2 * h * share : (2 * h + 1) * share]
        odd_block = turned[(2 * h + 1) * share : (2 * h + 2) * share]
        send_ref[h, :share, :] = jnp.where(odd, even_block, odd_block)
        keep_ref[h, :share, :] = jnp.where(odd, odd_block, even_block)
        send_ref[h, share:, :] = extra
        keep_ref[h, share:, :] = extra


def head_add_kernel(bit, keep_ref, came_ref, send_ref, next_ref):
    mine = (lax.axis_index("head") >> bit) & 1
    for out, which in ((send_ref, 1 - mine), (next_ref, mine)):
        for i in range(out.shape[0]):
            total = keep_ref[2 * i + which].astype(F32) + came_ref[2 * i + which].astype(F32)
            out[i] = total.astype(out.dtype)


def head_finish_kernel(keep_ref, came_ref, gain_ref, inverse_ref, x_ref, gy_ref, gx_ref, halo_ref, gain_out_ref):
    share = gx_ref.shape[0]
    total = keep_ref[0].astype(F32) + came_ref[0].astype(F32)
    mean = (total[share : share + 1] + total[share + 8 : share + 9]) / (share * lax.axis_size("head"))
    x, gy, inverse = x_ref[...].astype(F32), gy_ref[...].astype(F32), inverse_ref[:1, :]
    grad = total[:share]
    scaled = grad * gain_ref[:, :1]
    gx = (gy + inverse * (scaled - x * inverse * inverse * mean)).astype(BF16)
    gx_ref[...] = gx
    halo_ref[...] = gx[:, :TILE]
    column = jnp.sum(grad * x * inverse, axis=1, keepdims=True)
    spread = jnp.broadcast_to(column, (share, TILE))
    spread = jnp.concatenate([spread, jnp.zeros((-share % TILE, TILE), F32)], axis=0)
    gain_out_ref[...] = jnp.transpose(spread)[:8]


def merge_kernel(gx_ref, came_ref, ids_ref, out_ref, token_ref):
    tiles = gx_ref.shape[1] // TILE
    _, counts = window_rows(ids_ref, tiles)
    gx = [gx_ref[:, span(t)].astype(F32) for t in range(tiles)]
    gx[-1] = jnp.where(counts[-1], gx[-1], came_ref[...].astype(F32))
    for t in range(tiles - 1):
        out_ref[:, span(t)] = half_shifted(gx[t], gx[t + 1]).astype(BF16)
    token_ref[...] = jnp.zeros(token_ref.shape, F32)


def gain_add_kernel(own_ref, came_ref, out_ref):
    out_ref[...] = own_ref[...] + came_ref[...]


def swap(block, axis, distance):
    devices = range(lax.axis_size(axis))
    return lax.ppermute(block, axis, [(i, i ^ distance) for i in devices])


def shift(block, axis, by):
    count = lax.axis_size(axis)
    return lax.ppermute(block, axis, [(i, i + by) for i in range(count) if 0 <= i + by < count])


def per_device(patches, norm_gain, w_qkv, w_out, grad_y, window_ids):
    rows, features = patches.shape
    count = lax.axis_size("vis")
    levels = count.bit_length() - 1
    heads_axis = lax.axis_size("head")
    share = features // heads_axis
    part = features // count

    w_t = jnp.transpose(w_qkv, (1, 2, 0))
    wo_t = jnp.transpose(w_out)
    gain = norm_gain.reshape(-1, TILE)
    ids = window_ids.reshape(-1, TILE)
    hbm = lambda t: pltpu.with_memory_space_constraint(t, pltpu.HBM)
    edge_rows = call(
        halo_rows_kernel, [shape((2 * WIN, features))], hbm(patches), hbm(grad_y), weight=1,
        own_copies=(0, 1), scratch_shapes=[pltpu.SemaphoreType.DMA((2,))],
    )
    edge = shift(edge_rows[0], "vis", 1)
    places = rows + TILE
    columns, slim, pair = (features, places), (share, places), (2, share, places)
    (normed, grad_y_t, inverse, x_own, grad_y_own, own_gain, first_rows,
     kv, attended, grad_q, grad_kv, w_here, wo_here) = call(
        own_kernel,
        [shape(columns), shape(columns), shape((8, places), F32), shape(slim), shape(slim),
         shape((share, TILE), F32), shape((2 * WIN, features)),
         shape(pair), shape(slim), shape(slim), shape(pair, F32), shape(w_t.shape), shape(wo_t.shape)],
        hbm(patches), hbm(gain), hbm(w_t), hbm(grad_y), hbm(wo_t), ids,
        weight=1, own_copies=(0, 1, 2, 3, 4),
        scratch_shapes=[
            pltpu.VMEM((places, features), BF16), pltpu.VMEM(gain.shape, F32),
            pltpu.VMEM((places, features), BF16), pltpu.VMEM(columns, BF16),
            pltpu.VMEM((features, TILE), F32), pltpu.VMEM(slim, BF16), pltpu.VMEM(slim, BF16),
            pltpu.VMEM((2, share // HEAD_DIM, places, HEAD_DIM), BF16), pltpu.SemaphoreType.DMA((5,)),
        ],
    )
    (attended, grad_q, grad_kv, normed_halo, grad_y_halo, inverse, x_own, grad_y_own) = call(
        halo_kernel,
        [shape(slim), shape(slim), shape(pair), shape((features, TILE)), shape((features, TILE)),
         shape((8, places), F32), shape(slim), shape(slim)],
        edge, first_rows, gain, w_here, wo_here, ids, kv, attended, grad_q, grad_kv,
        inverse, x_own, grad_y_own,
        weight=1,
        scratch_shapes=[
            pltpu.VMEM((2, TILE, features), BF16), pltpu.VMEM((features, TILE), BF16),
            pltpu.VMEM((2, share, 2 * TILE), BF16),
            pltpu.VMEM((2, share // HEAD_DIM, 2 * TILE, HEAD_DIM), BF16),
        ],
    )

    rest = list(range(3, levels))
    if levels < 3:
        orders_first = orders_second = [list(range(levels))]
    else:
        orders_first = [[1, 0, 2] + rest, [0, 2, 1] + rest]
        orders_second = [[1, 0, 2] + rest, [0, 1, 2] + rest]
    every = list(range(levels - 1, -1, -1))
    sub = part // len(orders_first)
    bits = lambda orders, step: [order[step] for order in orders]

    def exchange(parts, orders, step):
        return [
            (keep, swap(send, "vis", 1 << bit))
            for send, keep, bit in zip(parts[::2], parts[1::2], bits(orders, step))
        ]

    def add(pairs, orders, step, weight, after=()):
        lefts = [[b for b in every if b not in order[:step]] for order in orders]
        return exchange(add_split(sub, lefts, bits(orders, step), pairs, after, weight), orders, step)

    parts = out_query_product(
        part, every, bits(orders_first, 0), grad_y_t, grad_y_halo, attended, normed, normed_halo, grad_q
    )
    first = exchange(parts, orders_first, 0)
    parts = pair_product(
        part, every, bits(orders_second, 0), normed, normed_halo, grad_kv, parts[:1]
    )
    second = exchange(parts, orders_second, 0)

    block = (heads_axis // 2, share + 16, places)
    send, keep = call(
        normed_grad_kernel, [shape(block), shape(block)],
        grad_q, grad_kv, w_here, gain, patches, edge, after=parts[:1],
    )
    tokens = []
    for step in range(1, levels):
        first = add(first, orders_first, step, WEIGHT if step == 1 else 1)
        tokens.append(first[0][:1])
        second = add(second, orders_second, step, WEIGHT, after=tokens[-1])
        tokens.append(second[0][:1])
    tokens = iter([()] + tokens[1:])
    for bit in range(1, heads_axis.bit_length() - 1):
        came = swap(send, "head", 1 << (bit - 1))
        block = (keep.shape[0] // 2,) + keep.shape[1:]
        send, keep = call(
            functools.partial(head_add_kernel, bit), [shape(block), shape(block, F32)], keep, came,
            after=next(tokens, ()),
        )
    came = swap(send, "head", heads_axis // 2)
    grad_x, grad_x_halo, grad_gain = call(
        head_finish_kernel,
        [shape(slim), shape((share, TILE)), shape((8, share + -share % TILE), F32)],
        keep, came, own_gain, inverse, x_own, grad_y_own, after=next(tokens, ()),
    )
    grad_x, token = call(
        merge_kernel, [shape((share, rows)), shape((8, TILE), F32)],
        grad_x, shift(grad_x_halo, "vis", -1), ids, weight=1,
    )
    for i, bit in enumerate(sorted(range(levels), key=lambda bit: (bit != 2, bit))):
        came = swap(grad_gain, "vis", 1 << bit)
        (grad_gain,) = call(
            gain_add_kernel, [shape(grad_gain.shape, F32)], grad_gain, came,
            weight=1, after=(*next(tokens, ()), *((token,) if i == 0 else ())),
        )
    grad_gain = grad_gain[0, :share]
    flat = lambda pairs: [t for pair in pairs for t in pair]
    grad_out, query_part = call(
        finish_out_query_kernel, [shape((part, share), F32)] * 2, *flat(first), weight=10 * WEIGHT
    )
    (grad_qkv,) = call(
        finish_kernel, [shape((3, part, share), F32)], query_part, *flat(second)
    )
    return jnp.transpose(grad_x), jnp.transpose(grad_qkv, (1, 0, 2)), grad_out, grad_gain


def solution(mesh):
    in_specs = (P("vis", None), P(), P(None, None, "head"), P(None, "head"), P("vis", None), P())
    out_specs = (P("vis", "head"), P("vis", None, "head"), P("vis", "head"), P("head"))
    return jax.shard_map(
        per_device, mesh=mesh, in_specs=in_specs, out_specs=out_specs, check_vma=False
    )
```

time: 261 us -> 67.9 us (0.26)
  waiting for transfers between devices: 162 us -> 15.4 us
  matrix products: 24.7 us -> 0 us
  blocking collectives: 22 us -> 0 us
  Pallas kernels: 0 us -> 20.2 us
  starting transfers between devices: 12.8 us -> 30.8 us
  between operations: 15.8 us -> 0.77 us
  other arithmetic: 11.8 us -> 0 us
  local copies, waits for them, and re-layouts: 11.8 us -> 0.61 us
    reduce_scatter x1 -> x0, waiting for transfers between devices: 115 us -> none  [per_device(): lax.psum_scatter(qkv_local, 'vis', scatter_dimension=0, tiled=True)]
    psum x1 -> x0, waiting for transfers between devices: 26.6 us -> none  [per_device(): lax.psum(partial_normed.astype(jnp.bfloat16), 'head').astype(jnp.float32)]
    psum x1 -> x0, blocking collectives: 22 us -> none  [per_device(): grad_gain = lax.psum(gain_part, 'vis')]
    dot_general x10 -> x0, matrix products: 21.2 us -> none  [the longest x1 5.52 us: per_device(): jnp.einsum('rd,rcj->dcj', normed, grad_proj, preferred_element_type=f32)]
    pallas_call x0 -> x18, Pallas kernels: none -> 20.2 us  [call(): pl.pallas_call(kernel, in_specs=specs, out_shape=outs, compiler_params=pl...]
    ppermute x4 -> x18, starting transfers between devices: 12.5 us -> 30.8 us  [the longest x16 24.7 us: swap(): return lax.ppermute(block, axis, [(i, i ^ distance) for i in devices])]
    unnamed x4 -> x0, waiting for transfers between devices: 10.8 us -> none
    ppermute x4 -> x18, waiting for transfers between devices: 9.18 us -> 15.4 us  [the longest x16 14 us: swap(): return lax.ppermute(block, axis, [(i, i ^ distance) for i in devices])]
  transfers between devices with their start and end apart: 7 -> 18, of which waited for: 5 -> 8; matrix products, arithmetic and copies ran while one was open for 8% -> 0% of each run, Pallas kernels for 0% -> 22%
where the time goes in v1:
time: 67.9 us; the launch traced here: 67.7 us
  starting transfers between devices  30.8 us (45%)
  Pallas kernels  20.2 us (30%)
  waiting for transfers between devices  15.4 us (23%)
  between operations  0.77 us (1%)
    ppermute x16, starting transfers between devices, swap(): return lax.ppermute(block, axis, [(i, i ^ distance) for i in devices])  24.7 us
    pallas_call x18, Pallas kernels, call(): pl.pallas_call(kernel, in_specs=specs, out_shape=outs, compiler_params=pl...  20.2 us
    ppermute x16, waiting for transfers between devices, swap(): return lax.ppermute(block, axis, [(i, i ^ distance) for i in devices])  14 us
    ppermute x2, starting transfers between devices, shift(): lax.ppermute(block, axis, [(i, i + by) for i in range(count) if 0 <= i +...  6.14 us
    ppermute x2, waiting for transfers between devices, shift(): lax.ppermute(block, axis, [(i, i + by) for i in range(count) if 0 <= i +...  1.38 us
  transfers between devices with their start and end apart: 18, of which 8 were waited for; matrix products, arithmetic and copies ran while one was open for 0% of the time, Pallas kernels for 22%

profile of v1, /device:TPU:0, one launch (start us, length us, event | category | flops | bytes accessed | tf_op | source)
XLA Modules:
  0.0 67.7 jit_solution(8586864258764371341)
XLA Ops:
  0.6 0.0 copy-start.1
  0.6 1.0 %shard_map.93 = bf16[128,1280]{1,0:T(8,128)(2,1)S(1)} custom-call(bf16[384,1280]{1,0:T(8,128)(2,1)} %refs_4_.1, bf16[384,1280]{1,0:T(8,128)(2,1)} %gy_any.3), custom_call_target="tpu_custom_call" | custom-call | flops 22937600 | bytes 2293760 | tf_op jit(solution)/shard_map/pallas_call | solution.py:41
  1.7 4.9 %collective-permute-start = (bf16[128,1280]{1,0:T(8,128)(2,1)S(1)}, bf16[128,1280]{1,0:T(8,128)(2,1)S(1)}, u32[]{:S(2)}, u32[]{:S(2)}) collective-permute-start(bf16[128,1280]{1,0:T(8,128)(2,1)S(1)} %shard_map.93), channel_id=1, source_target_pairs={{0,4},{4,8},{8,12},{12,16},{16,20},{20,24},{24,28},{1,5},{5,9},{9,... | collective-permute-start | bytes 983048 | tf_op jit(solution)/shard_map/ppermute | solution.py:497
  6.5 0.0 copy-done.1
  6.5 0.0 copy-start.2
  6.6 7.7 %shard_map.94 = (bf16[1280,512]{1,0:T(8,128)(2,1)S(1)}, bf16[1280,512]{1,0:T(8,128)(2,1)S(1)}, f32[8,512]{1,0:T(8,128)S(1)}, bf16[320,512]{1,0:T(8,128)(2,1)S(1)...) custom-call(bf16[384,1280]{1,0:T(8,128)(2,1)} %refs_4_.1, ...), custom_call_target="tpu_custom_call" | custom-call | flops 149432320 | bytes 14943232 | tf_op jit(solution)/shard_map/pallas_call | solution.py:41
  14.3 0.0 collective-permute-done.edge_ref.refs_5_
  14.3 0.0 copy-done.2
  14.3 2.4 %shard_map.95 = (bf16[320,512]{1,0:T(8,128)(2,1)S(1)}, bf16[320,512]{1,0:T(8,128)(2,1)S(1)}, bf16[2,320,512]{2,1,0:T(8,128)(2,1)S(1)}, bf16[1280,128]{1,0:T(8,12...) custom-call(bf16[128,1280]{1,0:T(8,128)(2,1)S(1)} %collective-permut, ...), custom_call_target="tpu_custom_call" | custom-call | flops 98805760 | bytes 9880576 | tf_op jit(solution)/shard_map/pallas_call | solution.py:41
  16.7 1.5 %shard_map.96 = (bf16[320,640]{1,0:T(8,128)(2,1)S(1)}, f32[320,640]{1,0:T(8,128)S(1)}, bf16[320,640]{1,0:T(8,128)(2,1)S(1)}, f32[320,640]{1,0:T(8,128)S(1)}) custom-call(bf16[1280,512]{1,0:T(8,128)(2,1)S(1)} %get-tuple-element.72.a_ref, bf16[1280,128]{1,0:T(8,128)(2,1)S(1)} %get-tuple-element.73.a_halo_ref, bf16[320,512]{1,0:T(8,128)(2,1)S(1)} %get-tuple-element.74.b_ref, ...), custom_call_target="tpu_custom_call" | custom-call | flops 19169280000 | bytes 1916928000 | tf_op jit(solution)/shard_map/pallas_call | solution.py:41
  18.2 1.7 %collective-permute-start.6 = (bf16[320,640]{1,0:T(8,128)(2,1)S(1)}, bf16[320,640]{1,0:T(8,128)(2,1)S(1)}, u32[]{:S(2)}, u32[]{:S(2)}) collective-permute-start(bf16[320,640]{1,0:T(8,128)(2,1)S(1)} %get-tuple-element.90), channel_id=1, source_target_pairs={{0,4},{4,0},{8,12},{12,8},{16,20},{20,16},{24,28},{28,24},{1,5},{5... | collective-permute-start | bytes 1228808 | tf_op jit(solution)/shard_map/ppermute | solution.py:492
  20.0 1.6 %collective-permute-start.5 = (bf16[320,640]{1,0:T(8,128)(2,1)S(1)}, bf16[320,640]{1,0:T(8,128)(2,1)S(1)}, u32[]{:S(2)}, u32[]{:S(2)}) collective-permute-start(bf16[320,640]{1,0:T(8,128)(2,1)S(1)} %get-tuple-element.75.refs_3_), channel_id=1, source_target_pairs={{0,8},{4,12},{8,0},{12,4},{16,24},{20,28},{24,16},{28,20},{1,9},{5... | collective-permute-start | bytes 1228808 | tf_op jit(solution)/shard_map/ppermute | solution.py:492
  21.6 0.0 copy-start
  21.6 1.2 %shard_map.97 = (bf16[320,640]{1,0:T(8,128)(2,1)S(1)}, f32[320,640]{1,0:T(8,128)S(1)}, bf16[320,640]{1,0:T(8,128)(2,1)S(1)}, f32[320,640]{1,0:T(8,128)S(1)}) custom-call(bf16[1280,512]{1,0:T(8,128)(2,1)S(1)} %get-tuple-element.70.c_ref.refs_0_, bf16[1280,128]{1,0:T(8,128)(2,1)S(1)} %get-tuple-element.71.c_halo_ref.refs_1_, ...), custom_call_target="tpu_custom_call" | custom-call | flops 14254080000 | bytes 1425408000 | tf_op jit(solution)/shard_map/pallas_call | solution.py:41
  22.8 1.5 %collective-permute-start.4 = (bf16[320,640]{1,0:T(8,128)(2,1)S(1)}, bf16[320,640]{1,0:T(8,128)(2,1)S(1)}, u32[]{:S(2)}, u32[]{:S(2)}) collective-permute-start(bf16[320,640]{1,0:T(8,128)(2,1)S(1)} %get-tuple-element.87), channel_id=1, source_target_pairs={{0,4},{4,0},{8,12},{12,8},{16,20},{20,16},{24,28},{28,24},{1,5},{5... | collective-permute-start | bytes 1228808 | tf_op jit(solution)/shard_map/ppermute | solution.py:492
  24.3 0.0 collective-permute-start.3
  24.3 0.0 copy-done
  24.3 2.5 %shard_map.98 = (bf16[2,336,512]{2,1,0:T(8,128)(2,1)S(1)}, bf16[2,336,512]{2,1,0:T(8,128)(2,1)S(1)}) custom-call(bf16[320,512]{1,0:T(8,128)(2,1)S(1)} %get-tuple-element.68.d_ref.refs_0_, bf16[2,320,512]{2,1,0:T(8,128)(2,1)S(1)} %get-tuple-element.69.refs_2_.refs_1_, bf16[3,320,1280]{2,1,0:T(8,128)(2,1)S(1)} %get-tuple-element.59.w_ref.refs_2_, ...), custom_call_target="tpu_custom_call" | custom-call | flops 18398208000 | bytes 1839820800 | tf_op jit(solution)/shard_map/pallas_call | solution.py:41
  26.8 0.1 collective-permute-start.1
  26.9 3.8 %collective-permute-done.6.refs_3_ = bf16[320,640]{1,0:T(8,128)(2,1)S(1)} collective-permute-done((bf16[320,640]{1,0:T(8,128)(2,1)S(1)}, bf16[320,640]{1,0:T(8,128)(2,1)S(1)}, u32[]{:S(2)}, u32[]{:S(2)}) %collective-permute-start.6) | collective-permute-done | bytes 409632 | tf_op jit(solution)/shard_map/ppermute | solution.py:492
  30.7 1.7 %collective-permute-done.5.refs_1_ = bf16[320,640]{1,0:T(8,128)(2,1)S(1)} collective-permute-done((bf16[320,640]{1,0:T(8,128)(2,1)S(1)}, bf16[320,640]{1,0:T(8,128)(2,1)S(1)}, u32[]{:S(2)}, u32[]{:S(2)}) %collective-permute-start.5) | collective-permute-done | bytes 409632 | tf_op jit(solution)/shard_map/ppermute | solution.py:492
  32.4 0.2 shard_map.100
  32.5 1.1 %collective-permute-start.8 = (bf16[160,640]{1,0:T(8,128)(2,1)S(1)}, bf16[160,640]{1,0:T(8,128)(2,1)S(1)}, u32[]{:S(2)}, u32[]{:S(2)}) collective-permute-start(bf16[160,640]{1,0:T(8,128)(2,1)S(1)} %get-tuple-element.96), channel_id=1, source_target_pairs={{0,4},{4,0},{8,12},{12,8},{16,20},{20,16},{24,28},{28,24},{1,5},{5... | collective-permute-start | bytes 614408 | tf_op jit(solution)/shard_map/ppermute | solution.py:492
  33.6 4.2 %collective-permute-start.9 = (bf16[160,640]{1,0:T(8,128)(2,1)S(1)}, bf16[160,640]{1,0:T(8,128)(2,1)S(1)}, u32[]{:S(2)}, u32[]{:S(2)}) collective-permute-start(bf16[160,640]{1,0:T(8,128)(2,1)S(1)} %get-tuple-element.98), channel_id=1, source_target_pairs={{0,16},{4,20},{8,24},{12,28},{16,0},{20,4},{24,8},{28,12},{1,17},{... | collective-permute-start | bytes 614408 | tf_op jit(solution)/shard_map/ppermute | solution.py:492
  37.8 0.0 collective-permute-done.1.came_ref
  37.8 0.1 shard_map.99
  37.9 1.6 %collective-permute-start.2 = (bf16[1,336,512]{2,1,0:T(8,128)(2,1)S(1)}, bf16[1,336,512]{2,1,0:T(8,128)(2,1)S(1)}, u32[]{:S(2)}, u32[]{:S(2)}) collective-permute-start(bf16[1,336,512]{2,1,0:T(8,128)(2,1)S(1)} %get-tuple-element.80), channel_id=1, source_target_pairs={{0,2},{1,3},{2,0},{3,1},{4,6},{5,7},{6,4},{7,5},{8,10},{9,11},{10,... | collective-permute-start | bytes 1032200 | tf_op jit(solution)/shard_map/ppermute | solution.py:492
  39.5 0.0 collective-permute-done.4.refs_3_
  39.5 4.0 %collective-permute-done.3.refs_1_ = bf16[320,640]{1,0:T(8,128)(2,1)S(1)} collective-permute-done((bf16[320,640]{1,0:T(8,128)(2,1)S(1)}, bf16[320,640]{1,0:T(8,128)(2,1)S(1)}, u32[]{:S(2)}, u32[]{:S(2)}) %collective-permute-start.3) | collective-permute-done | bytes 409632 | tf_op jit(solution)/shard_map/ppermute | solution.py:492
  43.5 0.2 shard_map.101
  43.7 1.0 %collective-permute-start.12 = (bf16[160,640]{1,0:T(8,128)(2,1)S(1)}, bf16[160,640]{1,0:T(8,128)(2,1)S(1)}, u32[]{:S(2)}, u32[]{:S(2)}) collective-permute-start(bf16[160,640]{1,0:T(8,128)(2,1)S(1)} %get-tuple-element.104), channel_id=1, source_target_pairs={{0,4},{4,0},{8,12},{12,8},{16,20},{20,16},{24,28},{28,24},{1,5},{5... | collective-permute-start | bytes 614408 | tf_op jit(solution)/shard_map/ppermute | solution.py:492
  44.7 0.0 collective-permute-start.13
  44.7 0.0 collective-permute-done.8.refs_1_
  44.7 0.3 collective-permute-done.9.refs_3_
  45.0 0.1 shard_map.104
  45.1 2.8 %collective-permute-start.10 = (bf16[80,640]{1,0:T(8,128)(2,1)S(1)}, bf16[80,640]{1,0:T(8,128)(2,1)S(1)}, u32[]{:S(2)}, u32[]{:S(2)}) collective-permute-start(bf16[80,640]{1,0:T(8,128)(2,1)S(1)} %get-tuple-element.100), channel_id=1, source_target_pairs={{0,16},{4,20},{8,24},{12,28},{16,0},{20,4},{24,8},{28,12},{1,17},{... | collective-permute-start | bytes 307208 | tf_op jit(solution)/shard_map/ppermute | solution.py:492
  47.9 4.1 %collective-permute-start.11 = (bf16[80,640]{1,0:T(8,128)(2,1)S(1)}, bf16[80,640]{1,0:T(8,128)(2,1)S(1)}, u32[]{:S(2)}, u32[]{:S(2)}) collective-permute-start(bf16[80,640]{1,0:T(8,128)(2,1)S(1)} %get-tuple-element.102), channel_id=1, source_target_pairs={{0,8},{4,12},{8,0},{12,4},{16,24},{20,28},{24,16},{28,20},{1,9},{5... | collective-permute-start | bytes 307208 | tf_op jit(solution)/shard_map/ppermute | solution.py:492
  52.0 0.0 collective-permute-done.2.refs_1_
  52.0 0.5 shard_map.102
  52.4 0.1 collective-permute-start.15
  52.5 0.0 collective-permute-done.12.refs_1_
  52.5 1.3 %collective-permute-start.7 = (bf16[320,128]{1,0:T(8,128)(2,1)S(1)}, bf16[320,128]{1,0:T(8,128)(2,1)S(1)}, u32[]{:S(2)}, u32[]{:S(2)}) collective-permute-start(bf16[320,128]{1,0:T(8,128)(2,1)S(1)} %get-tuple-element.94), channel_id=1, source_target_pairs={{4,0},{8,4},{12,8},{16,12},{20,16},{24,20},{28,24},{5,1},{9,5},{13... | collective-permute-start | bytes 245768 | tf_op jit(solution)/shard_map/ppermute | solution.py:497
  53.8 0.2 collective-permute-done.13.refs_3_
  54.0 0.1 shard_map.106
  54.1 3.3 %collective-permute-start.14 = (bf16[160,640]{1,0:T(8,128)(2,1)S(1)}, bf16[160,640]{1,0:T(8,128)(2,1)S(1)}, u32[]{:S(2)}, u32[]{:S(2)}) collective-permute-start(bf16[160,640]{1,0:T(8,128)(2,1)S(1)} %get-tuple-element.108), channel_id=1, source_target_pairs={{0,16},{4,20},{8,24},{12,28},{16,0},{20,4},{24,8},{28,12},{1,17},{... | collective-permute-start | bytes 614408 | tf_op jit(solution)/shard_map/ppermute | solution.py:492
  57.5 1.4 %collective-permute-done.7.came_ref = bf16[320,128]{1,0:T(8,128)(2,1)S(1)} collective-permute-done((bf16[320,128]{1,0:T(8,128)(2,1)S(1)}, bf16[320,128]{1,0:T(8,128)(2,1)S(1)}, u32[]{:S(2)}, u32[]{:S(2)}) %collective-permute-start.7) | collective-permute-done | bytes 81952 | tf_op jit(solution)/shard_map/ppermute | solution.py:497
  58.9 0.9 %shard_map.103 = (bf16[320,384]{1,0:T(8,128)(2,1)}, f32[8,128]{1,0:T(8,128)S(1)}) custom-call(bf16[320,512]{1,0:T(8,128)(2,1)S(1)} %get-tuple-element.93.gx_ref, bf16[320,128]{1,0:T(8,128)(2,1)S(1)} %collective-permute-done.7.came_ref, s32[24,128]{1,0:T(8,128)S(1)} %bitcast.8), custom_call_target="tpu_custom_call" | custom-call | flops 6717440 | bytes 671744 | tf_op jit(solution)/shard_map/pallas_call | solution.py:41
  59.7 0.0 collective-permute-done.15.refs_1_
  59.7 0.8 %collective-permute-start.16 = (f32[8,384]{1,0:T(8,128)S(1)}, f32[8,384]{1,0:T(8,128)S(1)}, u32[]{:S(2)}, u32[]{:S(2)}) collective-permute-start(f32[8,384]{1,0:T(8,128)S(1)} %shard_map.108.refs_0_), channel_id=1, source_target_pairs={{0,4},{4,0},{8,12},{12,8},{16,20},{20,16},{24,28},{28,24},{1,5},{5... | collective-permute-start | bytes 36872 | tf_op jit(solution)/shard_map/ppermute | solution.py:492
  60.5 0.0 collective-permute-done.10.refs_1_
  60.5 0.0 collective-permute-done.11.refs_3_
  60.5 0.8 %shard_map.105 = (f32[160,320]{1,0:T(8,128)}, f32[160,320]{1,0:T(8,128)S(1)}) custom-call(f32[80,640]{1,0:T(8,128)S(1)} %get-tuple-element.99.refs_0_.refs_4_.refs_2_, bf16[80,640]{1,0:T(8,128)(2,1)S(1)} %collective-permute-done.10.refs_1_, f32[80,640]{1,0:T(8,128)S(1)} %get-tuple-element.101.refs_2_, bf16[80,640]{1,0:T(8,128)(2,1)S(1)} %collective-permute-done.11.refs_3_), custom_call_target="tpu_custom_call" | custom-call | flops 30720000000 | bytes 3072000000 | tf_op jit(solution)/shard_map/pallas_call | solution.py:41
  61.3 2.1 %collective-permute-done.16.refs_1_ = f32[8,384]{1,0:T(8,128)S(1)} collective-permute-done((f32[8,384]{1,0:T(8,128)S(1)}, f32[8,384]{1,0:T(8,128)S(1)}, u32[]{:S(2)}, u32[]{:S(2)}) %collective-permute-start.16) | collective-permute-done | bytes 12320 | tf_op jit(solution)/shard_map/ppermute | solution.py:492
  63.4 0.9 %collective-permute-start.17 = (f32[8,384]{1,0:T(8,128)S(1)}, f32[8,384]{1,0:T(8,128)S(1)}, u32[]{:S(2)}, u32[]{:S(2)}) collective-permute-start(f32[8,384]{1,0:T(8,128)S(1)} %shard_map.109.own_ref), channel_id=1, source_target_pairs={{0,8},{4,12},{8,0},{12,4},{16,24},{20,28},{24,16},{28,20},{1,9},{5... | collective-permute-start | bytes 36872 | tf_op jit(solution)/shard_map/ppermute | solution.py:492
  64.3 0.0 collective-permute-done.14.refs_1_
  64.3 1.0 %shard_map.107 = f32[3,160,320]{2,1,0:T(8,128)} custom-call(f32[160,320]{1,0:T(8,128)S(1)} %get-tuple-element.103.query_ref, f32[160,640]{1,0:T(8,128)S(1)} %get-tuple-element.107.refs_0_.refs_2_, bf16[160,640]{1,0:T(8,128)(2,1)S(1)} %collective-permute-done.14.refs_1_), custom_call_target="tpu_custom_call" | custom-call | flops 4300800000 | bytes 430080000 | tf_op jit(solution)/shard_map/pallas_call | solution.py:41
  65.3 1.8 %collective-permute-done.17.came_ref = f32[8,384]{1,0:T(8,128)S(1)} collective-permute-done((f32[8,384]{1,0:T(8,128)S(1)}, f32[8,384]{1,0:T(8,128)S(1)}, u32[]{:S(2)}, u32[]{:S(2)}) %collective-permute-start.17) | collective-permute-done | bytes 12320 | tf_op jit(solution)/shard_map/ppermute | solution.py:492
  67.1 0.6 slice_reduce_fusion
  (3 shorter events, 0.0 us)
Async XLA Ops:
  0.6 5.9 %copy-start.1 = (s32[3072]{0:T(1024)S(1)}, s32[3072]{0:T(1024)}, u32[]{:S(2)}) copy-start(s32[3072]{0:T(1024)} %param.11) | copy-start | bytes 36868
  1.7 12.6 %collective-permute-start = (bf16[128,1280]{1,0:T(8,128)(2,1)S(1)}, bf16[128,1280]{1,0:T(8,128)(2,1)S(1)}, u32[]{:S(2)}, u32[]{:S(2)}) collective-permute-start(bf16[128,1280]{1,0:T(8,128)(2,1)S(1)} %shard_map.93), channel_id=1, source_target_pairs={{0,4},{4,8},{8,12},{12,16},{16,20},{20,24},{24,28},{1,5},{5,9},{9,... | collective-permute-start | bytes 983048 | tf_op jit(solution)/shard_map/ppermute | solution.py:497
  6.5 7.7 %copy-start.2 = (f32[1280]{0:T(1024)S(1)}, f32[1280]{0:T(1024)}, u32[]{:S(2)}) copy-start(f32[1280]{0:T(1024)} %param.7) | copy-start | bytes 15364
  18.2 12.5 %collective-permute-start.6 = (bf16[320,640]{1,0:T(8,128)(2,1)S(1)}, bf16[320,640]{1,0:T(8,128)(2,1)S(1)}, u32[]{:S(2)}, u32[]{:S(2)}) collective-permute-start(bf16[320,640]{1,0:T(8,128)(2,1)S(1)} %get-tuple-element.90), channel_id=1, source_target_pairs={{0,4},{4,0},{8,12},{12,8},{16,20},{20,16},{24,28},{28,24},{1,5},{5... | collective-permute-start | bytes 1228808 | tf_op jit(solution)/shard_map/ppermute | solution.py:492
  20.0 12.4 %collective-permute-start.5 = (bf16[320,640]{1,0:T(8,128)(2,1)S(1)}, bf16[320,640]{1,0:T(8,128)(2,1)S(1)}, u32[]{:S(2)}, u32[]{:S(2)}) collective-permute-start(bf16[320,640]{1,0:T(8,128)(2,1)S(1)} %get-tuple-element.75.refs_3_), channel_id=1, source_target_pairs={{0,8},{4,12},{8,0},{12,4},{16,24},{20,28},{24,16},{28,20},{1,9},{5... | collective-permute-start | bytes 1228808 | tf_op jit(solution)/shard_map/ppermute | solution.py:492
  21.6 2.7 %copy-start = (bf16[384,1280]{1,0:T(8,128)(2,1)S(1)}, bf16[384,1280]{1,0:T(8,128)(2,1)}, u32[]{:S(2)}) copy-start(bf16[384,1280]{1,0:T(8,128)(2,1)} %refs_4_.1) | copy-start | bytes 2949124
  22.8 16.8 %collective-permute-start.4 = (bf16[320,640]{1,0:T(8,128)(2,1)S(1)}, bf16[320,640]{1,0:T(8,128)(2,1)S(1)}, u32[]{:S(2)}, u32[]{:S(2)}) collective-permute-start(bf16[320,640]{1,0:T(8,128)(2,1)S(1)} %get-tuple-element.87), channel_id=1, source_target_pairs={{0,4},{4,0},{8,12},{12,8},{16,20},{20,16},{24,28},{28,24},{1,5},{5... | collective-permute-start | bytes 1228808 | tf_op jit(solution)/shard_map/ppermute | solution.py:492
  24.3 19.3 %collective-permute-start.3 = (bf16[320,640]{1,0:T(8,128)(2,1)S(1)}, bf16[320,640]{1,0:T(8,128)(2,1)S(1)}, u32[]{:S(2)}, u32[]{:S(2)}) collective-permute-start(bf16[320,640]{1,0:T(8,128)(2,1)S(1)} %get-tuple-element.76.refs_6_), channel_id=1, source_target_pairs={{0,8},{4,12},{8,0},{12,4},{16,24},{20,28},{24,16},{28,20},{1,9},{5... | collective-permute-start | bytes 1228808 | tf_op jit(solution)/shard_map/ppermute | solution.py:492
  26.8 11.0 %collective-permute-start.1 = (bf16[2,336,512]{2,1,0:T(8,128)(2,1)S(1)}, bf16[2,336,512]{2,1,0:T(8,128)(2,1)S(1)}, u32[]{:S(2)}, u32[]{:S(2)}) collective-permute-start(bf16[2,336,512]{2,1,0:T(8,128)(2,1)S(1)} %get-tuple-element.78), channel_id=1, source_target_pairs={{0,1},{1,0},{2,3},{3,2},{4,5},{5,4},{6,7},{7,6},{8,9},{9,8},{10,11... | collective-permute-start | bytes 2064392 | tf_op jit(solution)/shard_map/ppermute | solution.py:492
  32.5 12.2 %collective-permute-start.8 = (bf16[160,640]{1,0:T(8,128)(2,1)S(1)}, bf16[160,640]{1,0:T(8,128)(2,1)S(1)}, u32[]{:S(2)}, u32[]{:S(2)}) collective-permute-start(bf16[160,640]{1,0:T(8,128)(2,1)S(1)} %get-tuple-element.96), channel_id=1, source_target_pairs={{0,4},{4,0},{8,12},{12,8},{16,20},{20,16},{24,28},{28,24},{1,5},{5... | collective-permute-start | bytes 614408 | tf_op jit(solution)/shard_map/ppermute | solution.py:492
  33.6 11.4 %collective-permute-start.9 = (bf16[160,640]{1,0:T(8,128)(2,1)S(1)}, bf16[160,640]{1,0:T(8,128)(2,1)S(1)}, u32[]{:S(2)}, u32[]{:S(2)}) collective-permute-start(bf16[160,640]{1,0:T(8,128)(2,1)S(1)} %get-tuple-element.98), channel_id=1, source_target_pairs={{0,16},{4,20},{8,24},{12,28},{16,0},{20,4},{24,8},{28,12},{1,17},{... | collective-permute-start | bytes 614408 | tf_op jit(solution)/shard_map/ppermute | solution.py:492
  37.9 14.0 %collective-permute-start.2 = (bf16[1,336,512]{2,1,0:T(8,128)(2,1)S(1)}, bf16[1,336,512]{2,1,0:T(8,128)(2,1)S(1)}, u32[]{:S(2)}, u32[]{:S(2)}) collective-permute-start(bf16[1,336,512]{2,1,0:T(8,128)(2,1)S(1)} %get-tuple-element.80), channel_id=1, source_target_pairs={{0,2},{1,3},{2,0},{3,1},{4,6},{5,7},{6,4},{7,5},{8,10},{9,11},{10,... | collective-permute-start | bytes 1032200 | tf_op jit(solution)/shard_map/ppermute | solution.py:492
  43.7 8.8 %collective-permute-start.12 = (bf16[160,640]{1,0:T(8,128)(2,1)S(1)}, bf16[160,640]{1,0:T(8,128)(2,1)S(1)}, u32[]{:S(2)}, u32[]{:S(2)}) collective-permute-start(bf16[160,640]{1,0:T(8,128)(2,1)S(1)} %get-tuple-element.104), channel_id=1, source_target_pairs={{0,4},{4,0},{8,12},{12,8},{16,20},{20,16},{24,28},{28,24},{1,5},{5... | collective-permute-start | bytes 614408 | tf_op jit(solution)/shard_map/ppermute | solution.py:492
  44.7 9.3 %collective-permute-start.13 = (bf16[160,640]{1,0:T(8,128)(2,1)S(1)}, bf16[160,640]{1,0:T(8,128)(2,1)S(1)}, u32[]{:S(2)}, u32[]{:S(2)}) collective-permute-start(bf16[160,640]{1,0:T(8,128)(2,1)S(1)} %get-tuple-element.106), channel_id=1, source_target_pairs={{0,8},{4,12},{8,0},{12,4},{16,24},{20,28},{24,16},{28,20},{1,9},{5... | collective-permute-start | bytes 614408 | tf_op jit(solution)/shard_map/ppermute | solution.py:492
  45.1 15.4 %collective-permute-start.10 = (bf16[80,640]{1,0:T(8,128)(2,1)S(1)}, bf16[80,640]{1,0:T(8,128)(2,1)S(1)}, u32[]{:S(2)}, u32[]{:S(2)}) collective-permute-start(bf16[80,640]{1,0:T(8,128)(2,1)S(1)} %get-tuple-element.100), channel_id=1, source_target_pairs={{0,16},{4,20},{8,24},{12,28},{16,0},{20,4},{24,8},{28,12},{1,17},{... | collective-permute-start | bytes 307208 | tf_op jit(solution)/shard_map/ppermute | solution.py:492
  47.9 12.6 %collective-permute-start.11 = (bf16[80,640]{1,0:T(8,128)(2,1)S(1)}, bf16[80,640]{1,0:T(8,128)(2,1)S(1)}, u32[]{:S(2)}, u32[]{:S(2)}) collective-permute-start(bf16[80,640]{1,0:T(8,128)(2,1)S(1)} %get-tuple-element.102), channel_id=1, source_target_pairs={{0,8},{4,12},{8,0},{12,4},{16,24},{20,28},{24,16},{28,20},{1,9},{5... | collective-permute-start | bytes 307208 | tf_op jit(solution)/shard_map/ppermute | solution.py:492
  52.4 7.3 %collective-permute-start.15 = (f32[8,384]{1,0:T(8,128)S(1)}, f32[8,384]{1,0:T(8,128)S(1)}, u32[]{:S(2)}, u32[]{:S(2)}) collective-permute-start(f32[8,384]{1,0:T(8,128)S(1)} %get-tuple-element.110.refs_0_), channel_id=1, source_target_pairs={{0,16},{4,20},{8,24},{12,28},{16,0},{20,4},{24,8},{28,12},{1,17},{... | collective-permute-start | bytes 36872 | tf_op jit(solution)/shard_map/ppermute | solution.py:492
  52.5 6.3 %collective-permute-start.7 = (bf16[320,128]{1,0:T(8,128)(2,1)S(1)}, bf16[320,128]{1,0:T(8,128)(2,1)S(1)}, u32[]{:S(2)}, u32[]{:S(2)}) collective-permute-start(bf16[320,128]{1,0:T(8,128)(2,1)S(1)} %get-tuple-element.94), channel_id=1, source_target_pairs={{4,0},{8,4},{12,8},{16,12},{20,16},{24,20},{28,24},{5,1},{9,5},{13... | collective-permute-start | bytes 245768 | tf_op jit(solution)/shard_map/ppermute | solution.py:497
  54.1 10.2 %collective-permute-start.14 = (bf16[160,640]{1,0:T(8,128)(2,1)S(1)}, bf16[160,640]{1,0:T(8,128)(2,1)S(1)}, u32[]{:S(2)}, u32[]{:S(2)}) collective-permute-start(bf16[160,640]{1,0:T(8,128)(2,1)S(1)} %get-tuple-element.108), channel_id=1, source_target_pairs={{0,16},{4,20},{8,24},{12,28},{16,0},{20,4},{24,8},{28,12},{1,17},{... | collective-permute-start | bytes 614408 | tf_op jit(solution)/shard_map/ppermute | solution.py:492
  59.7 3.7 %collective-permute-start.16 = (f32[8,384]{1,0:T(8,128)S(1)}, f32[8,384]{1,0:T(8,128)S(1)}, u32[]{:S(2)}, u32[]{:S(2)}) collective-permute-start(f32[8,384]{1,0:T(8,128)S(1)} %shard_map.108.refs_0_), channel_id=1, source_target_pairs={{0,4},{4,0},{8,12},{12,8},{16,20},{20,16},{24,28},{28,24},{1,5},{5... | collective-permute-start | bytes 36872 | tf_op jit(solution)/shard_map/ppermute | solution.py:492
  63.4 3.7 %collective-permute-start.17 = (f32[8,384]{1,0:T(8,128)S(1)}, f32[8,384]{1,0:T(8,128)S(1)}, u32[]{:S(2)}, u32[]{:S(2)}) collective-permute-start(f32[8,384]{1,0:T(8,128)S(1)} %shard_map.109.own_ref), channel_id=1, source_target_pairs={{0,8},{4,12},{8,0},{12,4},{16,24},{20,28},{24,16},{28,20},{1,9},{5... | collective-permute-start | bytes 36872 | tf_op jit(solution)/shard_map/ppermute | solution.py:492

commit v2 on v1

--- a/solution.py
+++ b/solution.py
@@ -286,23 +286,24 @@
     return [[p + step * which for p in base] for which in (1 - mine, mine)]
 
 
-def gathered(own_ref, halo_ref, scratch, part, left, bits):
+def gathered(own_ref, halo_ref, scratch, part, left, bits, sides=(0, 1)):
     sub = part // len(bits)
     to = 0
     for chain, bit in enumerate(bits):
-        for side in side_blocks(left, bit):
-            for p in side:
+        blocks = side_blocks(left, bit)
+        for side in sides:
+            for p in blocks[side]:
                 at = pl.ds(pl.multiple_of(p * part + chain * sub, 16), sub)
                 scratch[to : to + sub, :TILE] = halo_ref[at, :]
                 scratch[to : to + sub, TILE:] = own_ref[at, TILE:]
                 to += sub
 
 
-def out_query_product_kernel(part, left, bits, a_ref, a_halo_ref, b_ref, c_ref, c_halo_ref, d_ref, *refs):
+def out_query_product_kernel(part, left, bits, side, a_ref, a_halo_ref, b_ref, c_ref, c_halo_ref, d_ref, *refs):
     outs, (a_rows, c_rows) = refs[:-2], refs[-2:]
     share, rows = b_ref.shape
-    gathered(a_ref, a_halo_ref, a_rows, part, left, bits)
-    gathered(c_ref, c_halo_ref, c_rows, part, left, bits)
+    gathered(a_ref, a_halo_ref, a_rows, part, left, bits, (side,))
+    gathered(c_ref, c_halo_ref, c_rows, part, left, bits, (side,))
     gap = jnp.zeros((-share % TILE, rows), BF16)
     b = jnp.transpose(jnp.concatenate([b_ref[...], gap], axis=0))
     d = jnp.transpose(jnp.concatenate([gap, d_ref[...]], axis=0))
@@ -359,18 +360,19 @@
     return [shape((rows // 2, width)), shape((rows // 2, width), F32)] * chains
 
 
-def out_query_product(part, left, bits, a, a_halo, b, c, c_halo, d):
+def out_query_product(part, left, bits, a, a_halo, b, c, c_halo, d, side, after=()):
     features = a.shape[0]
     share, rows = b.shape
     if part % (16 * len(bits)):
         a = jnp.concatenate([a_halo, a[:, TILE:]], axis=1)
         c = jnp.concatenate([c_halo, c[:, TILE:]], axis=1)
         product = jnp.concatenate([dot(a, b, NT), dot(c, d, NT)], axis=1)
-        return split_product(product, part, left, bits)
+        return split_product(product, part, left, bits)[side::2]
     return call(
-        functools.partial(out_query_product_kernel, part, left, bits),
-        halves(features // len(bits), 2 * share, len(bits)), a, a_halo, b, c, c_halo, d,
-        scratch_shapes=[pltpu.VMEM((features, rows), BF16)] * 2,
+        functools.partial(out_query_product_kernel, part, left, bits, side),
+        halves(features // len(bits), 2 * share, len(bits))[side::2],
+        a, a_halo, b, c, c_halo, d, after=after, weight=1,
+        scratch_shapes=[pltpu.VMEM((features // 2, rows), BF16)] * 2,
     )
 
 
@@ -566,20 +568,23 @@
         lefts = [[b for b in every if b not in order[:step]] for order in orders]
         return exchange(add_split(sub, lefts, bits(orders, step), pairs, after, weight), orders, step)
 
-    parts = out_query_product(
-        part, every, bits(orders_first, 0), grad_y_t, grad_y_halo, attended, normed, normed_halo, grad_q
-    )
-    first = exchange(parts, orders_first, 0)
-    parts = pair_product(
-        part, every, bits(orders_second, 0), normed, normed_halo, grad_kv, parts[:1]
-    )
-    second = exchange(parts, orders_second, 0)
-
+    first_product = functools.partial(
+        out_query_product, part, every, bits(orders_first, 0),
+        grad_y_t, grad_y_halo, attended, normed, normed_halo, grad_q,
+    )
+    sends = first_product(0)
     block = (heads_axis // 2, share + 16, places)
     send, keep = call(
         normed_grad_kernel, [shape(block), shape(block)],
-        grad_q, grad_kv, w_here, gain, patches, edge, after=parts[:1],
-    )
+        grad_q, grad_kv, w_here, gain, patches, edge, after=sends[:1],
+    )
+    parts = pair_product(
+        part, every, bits(orders_second, 0), normed, normed_halo, grad_kv, (send,)
+    )
+    keeps = first_product(1, parts[:1])
+    first = exchange([t for pair in zip(sends, keeps) for t in pair], orders_first, 0)
+    second = exchange(parts, orders_second, 0)
+
     tokens = []
     for step in range(1, levels):
         first = add(first, orders_first, step, WEIGHT if step == 1 else 1)
@@ -608,7 +613,7 @@
         came = swap(grad_gain, "vis", 1 << bit)
         (grad_gain,) = call(
             gain_add_kernel, [shape(grad_gain.shape, F32)], grad_gain, came,
-            weight=1, after=(*next(tokens, ()), *((token,) if i == 0 else ())),
+            weight=1, after=(*next(tokens, ()), *((token,) if i == 2 else ())),
         )
     grad_gain = grad_gain[0, :share]
     flat = lambda pairs: [t for pair in pairs for t in pair]
@@ -616,7 +621,8 @@
         finish_out_query_kernel, [shape((part, share), F32)] * 2, *flat(first), weight=10 * WEIGHT
     )
     (grad_qkv,) = call(
-        finish_kernel, [shape((3, part, share), F32)], query_part, *flat(second)
+        finish_kernel, [shape((3, part, share), F32)], query_part, *flat(second),
+        after=(token, grad_gain),
     )
     return jnp.transpose(grad_x), jnp.transpose(grad_qkv, (1, 0, 2)), grad_out, grad_gain
 

time: 67.9 us -> 65.4 us (0.963)
  starting transfers between devices: 30.8 us -> 27.3 us
  waiting for transfers between devices: 15.4 us -> 16.5 us
    ppermute x16, starting transfers between devices: 24.7 us -> 21.2 us  [swap(): return lax.ppermute(block, axis, [(i, i ^ distance) for i in devices])]
    ppermute x16, waiting for transfers between devices: 14 us -> 16.5 us  [swap(): return lax.ppermute(block, axis, [(i, i ^ distance) for i in devices])]
    ppermute x2, waiting for transfers between devices: 1.38 us -> 0.01 us  [shift(): lax.ppermute(block, axis, [(i, i + by) for i in range(count) if 0 <= i +...]
    pallas_call x18 -> x19, Pallas kernels: 20.2 us -> 20.5 us  [call(): pl.pallas_call(kernel, in_specs=specs, out_shape=outs, compiler_params=pl...]
  transfers between devices with their start and end apart: 18 -> 18, of which waited for: 8 -> 8; matrix products, arithmetic and copies ran while one was open for 0% -> 0% of each run, Pallas kernels for 22% -> 23%
where the time goes in v2:
time: 65.4 us; the launch traced here: 65.2 us
  starting transfers between devices  27.3 us (42%)
  Pallas kernels  20.5 us (31%)
  waiting for transfers between devices  16.5 us (25%)
  between operations  0.81 us (1%)
    ppermute x16, starting transfers between devices, swap(): return lax.ppermute(block, axis, [(i, i ^ distance) for i in devices])  21.2 us
    pallas_call x19, Pallas kernels, call(): pl.pallas_call(kernel, in_specs=specs, out_shape=outs, compiler_params=pl...  20.5 us
    ppermute x16, waiting for transfers between devices, swap(): return lax.ppermute(block, axis, [(i, i ^ distance) for i in devices])  16.5 us
    ppermute x2, starting transfers between devices, shift(): lax.ppermute(block, axis, [(i, i + by) for i in range(count) if 0 <= i +...  6.14 us
  transfers between devices with their start and end apart: 18, of which 8 were waited for; matrix products, arithmetic and copies ran while one was open for 0% of the time, Pallas kernels for 23%

profile of v2, /device:TPU:0, one launch (start us, length us, event | category | flops | bytes accessed | tf_op | source)
XLA Modules:
  0.0 65.2 jit_solution(6828096059898949124)
XLA Ops:
  0.6 0.0 copy-start.1
  0.6 1.0 %shard_map.93 = bf16[128,1280]{1,0:T(8,128)(2,1)S(1)} custom-call(bf16[384,1280]{1,0:T(8,128)(2,1)} %refs_4_.1, bf16[384,1280]{1,0:T(8,128)(2,1)} %gy_any.3), custom_call_target="tpu_custom_call" | custom-call | flops 22937600 | bytes 2293760 | tf_op jit(solution)/shard_map/pallas_call | solution.py:41
  1.7 4.9 %collective-permute-start = (bf16[128,1280]{1,0:T(8,128)(2,1)S(1)}, bf16[128,1280]{1,0:T(8,128)(2,1)S(1)}, u32[]{:S(2)}, u32[]{:S(2)}) collective-permute-start(bf16[128,1280]{1,0:T(8,128)(2,1)S(1)} %shard_map.93), channel_id=1, source_target_pairs={{0,4},{4,8},{8,12},{12,16},{16,20},{20,24},{24,28},{1,5},{5,9},{9,... | collective-permute-start | bytes 983048 | tf_op jit(solution)/shard_map/ppermute | solution.py:499
  6.5 0.0 copy-done.1
  6.5 0.0 copy-start.2
  6.6 7.7 %shard_map.94 = (bf16[1280,512]{1,0:T(8,128)(2,1)S(1)}, bf16[1280,512]{1,0:T(8,128)(2,1)S(1)}, f32[8,512]{1,0:T(8,128)S(1)}, bf16[320,512]{1,0:T(8,128)(2,1)S(1)...) custom-call(bf16[384,1280]{1,0:T(8,128)(2,1)} %refs_4_.1, ...), custom_call_target="tpu_custom_call" | custom-call | flops 149432320 | bytes 14943232 | tf_op jit(solution)/shard_map/pallas_call | solution.py:41
  14.2 0.0 collective-permute-done.edge_ref.refs_5_
  14.3 0.0 copy-done.2
  14.3 2.4 %shard_map.95 = (bf16[320,512]{1,0:T(8,128)(2,1)S(1)}, bf16[320,512]{1,0:T(8,128)(2,1)S(1)}, bf16[2,320,512]{2,1,0:T(8,128)(2,1)S(1)}, bf16[1280,128]{1,0:T(8,12...) custom-call(bf16[128,1280]{1,0:T(8,128)(2,1)S(1)} %collective-permut, ...), custom_call_target="tpu_custom_call" | custom-call | flops 98805760 | bytes 9880576 | tf_op jit(solution)/shard_map/pallas_call | solution.py:41
  16.7 0.0 copy-start
  16.7 0.9 %shard_map.96 = (bf16[320,640]{1,0:T(8,128)(2,1)S(1)}, bf16[320,640]{1,0:T(8,128)(2,1)S(1)}) custom-call(bf16[1280,512]{1,0:T(8,128)(2,1)S(1)} %get-tuple-element.70.a_ref.refs_0_, bf16[1280,128]{1,0:T(8,128)(2,1)S(1)} %get-tuple-element.71.a_halo_ref.refs_1_, bf16[320,512]{1,0:T(8,128)(2,1)S(1)} %get-tuple-element.72.b_ref.refs_2_, ...), custom_call_target="tpu_custom_call" | custom-call | flops 47513600 | bytes 4751360 | tf_op jit(solution)/shard_map/pallas_call | solution.py:41
  17.6 1.7 %collective-permute-start.6 = (bf16[320,640]{1,0:T(8,128)(2,1)S(1)}, bf16[320,640]{1,0:T(8,128)(2,1)S(1)}, u32[]{:S(2)}, u32[]{:S(2)}) collective-permute-start(bf16[320,640]{1,0:T(8,128)(2,1)S(1)} %get-tuple-element.90), channel_id=1, source_target_pairs={{0,4},{4,0},{8,12},{12,8},{16,20},{20,16},{24,28},{28,24},{1,5},{5... | collective-permute-start | bytes 1228808 | tf_op jit(solution)/shard_map/ppermute | solution.py:494
  19.3 1.6 %collective-permute-start.5 = (bf16[320,640]{1,0:T(8,128)(2,1)S(1)}, bf16[320,640]{1,0:T(8,128)(2,1)S(1)}, u32[]{:S(2)}, u32[]{:S(2)}) collective-permute-start(bf16[320,640]{1,0:T(8,128)(2,1)S(1)} %get-tuple-element.75.refs_6_), channel_id=1, source_target_pairs={{0,8},{4,12},{8,0},{12,4},{16,24},{20,28},{24,16},{28,20},{1,9},{5... | collective-permute-start | bytes 1228808 | tf_op jit(solution)/shard_map/ppermute | solution.py:494
  20.9 0.0 copy-done
  20.9 2.5 %shard_map.97 = (bf16[2,336,512]{2,1,0:T(8,128)(2,1)S(1)}, bf16[2,336,512]{2,1,0:T(8,128)(2,1)S(1)}) custom-call(bf16[320,512]{1,0:T(8,128)(2,1)S(1)} %get-tuple-element.68.d_ref.refs_0_.refs_5_, bf16[2,320,512]{2,1,0:T(8,128)(2,1)S(1)} %get-tuple-element.69.refs_1_.refs_2_, bf16[3,320,1280]{2,1,0:T(8,128)(2,1)S(1)} %get-tuple-element.59.w_ref.refs_2_, ...), custom_call_target="tpu_custom_call" | custom-call | flops 18398208000 | bytes 1839820800 | tf_op jit(solution)/shard_map/pallas_call | solution.py:41
  23.4 0.1 collective-permute-start.1
  23.5 1.3 %shard_map.99 = (bf16[320,640]{1,0:T(8,128)(2,1)S(1)}, f32[320,640]{1,0:T(8,128)S(1)}, bf16[320,640]{1,0:T(8,128)(2,1)S(1)}, f32[320,640]{1,0:T(8,128)S(1)}) custom-call(bf16[1280,512]{1,0:T(8,128)(2,1)S(1)} %get-tuple-element.73.c_ref.refs_0_.refs_3_, bf16[1280,128]{1,0:T(8,128)(2,1)S(1)} %get-tuple-element.74.c_halo_ref.refs_1_.refs_4_, ...), custom_call_target="tpu_custom_call" | custom-call | flops 14254080000 | bytes 1425408000 | tf_op jit(solution)/shard_map/pallas_call | solution.py:41
  24.7 1.5 %collective-permute-start.4 = (bf16[320,640]{1,0:T(8,128)(2,1)S(1)}, bf16[320,640]{1,0:T(8,128)(2,1)S(1)}, u32[]{:S(2)}, u32[]{:S(2)}) collective-permute-start(bf16[320,640]{1,0:T(8,128)(2,1)S(1)} %get-tuple-element.87), channel_id=1, source_target_pairs={{0,4},{4,0},{8,12},{12,8},{16,20},{20,16},{24,28},{28,24},{1,5},{5... | collective-permute-start | bytes 1228808 | tf_op jit(solution)/shard_map/ppermute | solution.py:494
  26.2 0.0 collective-permute-start.3
  26.2 0.9 %shard_map.100 = (f32[320,640]{1,0:T(8,128)S(1)}, f32[320,640]{1,0:T(8,128)S(1)}) custom-call(bf16[1280,512]{1,0:T(8,128)(2,1)S(1)} %get-tuple-element.70.a_ref.refs_0_, bf16[1280,128]{1,0:T(8,128)(2,1)S(1)} %get-tuple-element.71.a_halo_ref.refs_1_, bf16[320,512]{1,0:T(8,128)(2,1)S(1)} %get-tuple-element.72.b_ref.refs_2_, ...), custom_call_target="tpu_custom_call" | custom-call | flops 55705600 | bytes 5570560 | tf_op jit(solution)/shard_map/pallas_call | solution.py:41
  27.1 2.0 %collective-permute-done.6.refs_3_ = bf16[320,640]{1,0:T(8,128)(2,1)S(1)} collective-permute-done((bf16[320,640]{1,0:T(8,128)(2,1)S(1)}, bf16[320,640]{1,0:T(8,128)(2,1)S(1)}, u32[]{:S(2)}, u32[]{:S(2)}) %collective-permute-start.6) | collective-permute-done | bytes 409632 | tf_op jit(solution)/shard_map/ppermute | solution.py:494
  29.2 1.6 %collective-permute-done.5.refs_1_ = bf16[320,640]{1,0:T(8,128)(2,1)S(1)} collective-permute-done((bf16[320,640]{1,0:T(8,128)(2,1)S(1)}, bf16[320,640]{1,0:T(8,128)(2,1)S(1)}, u32[]{:S(2)}, u32[]{:S(2)}) %collective-permute-start.5) | collective-permute-done | bytes 409632 | tf_op jit(solution)/shard_map/ppermute | solution.py:494
  30.8 0.3 shard_map.101
  31.1 1.4 %collective-permute-start.8 = (bf16[160,640]{1,0:T(8,128)(2,1)S(1)}, bf16[160,640]{1,0:T(8,128)(2,1)S(1)}, u32[]{:S(2)}, u32[]{:S(2)}) collective-permute-start(bf16[160,640]{1,0:T(8,128)(2,1)S(1)} %get-tuple-element.96), channel_id=1, source_target_pairs={{0,4},{4,0},{8,12},{12,8},{16,20},{20,16},{24,28},{28,24},{1,5},{5... | collective-permute-start | bytes 614408 | tf_op jit(solution)/shard_map/ppermute | solution.py:494
  32.5 2.6 %collective-permute-start.9 = (bf16[160,640]{1,0:T(8,128)(2,1)S(1)}, bf16[160,640]{1,0:T(8,128)(2,1)S(1)}, u32[]{:S(2)}, u32[]{:S(2)}) collective-permute-start(bf16[160,640]{1,0:T(8,128)(2,1)S(1)} %get-tuple-element.98), channel_id=1, source_target_pairs={{0,16},{4,20},{8,24},{12,28},{16,0},{20,4},{24,8},{28,12},{1,17},{... | collective-permute-start | bytes 614408 | tf_op jit(solution)/shard_map/ppermute | solution.py:494
  35.1 0.0 collective-permute-done.1.came_ref
  35.1 0.1 shard_map.98
  35.3 1.6 %collective-permute-start.2 = (bf16[1,336,512]{2,1,0:T(8,128)(2,1)S(1)}, bf16[1,336,512]{2,1,0:T(8,128)(2,1)S(1)}, u32[]{:S(2)}, u32[]{:S(2)}) collective-permute-start(bf16[1,336,512]{2,1,0:T(8,128)(2,1)S(1)} %get-tuple-element.79), channel_id=1, source_target_pairs={{0,2},{1,3},{2,0},{3,1},{4,6},{5,7},{6,4},{7,5},{8,10},{9,11},{10,... | collective-permute-start | bytes 1032200 | tf_op jit(solution)/shard_map/ppermute | solution.py:494
  36.9 1.1 %collective-permute-done.4.refs_3_ = bf16[320,640]{1,0:T(8,128)(2,1)S(1)} collective-permute-done((bf16[320,640]{1,0:T(8,128)(2,1)S(1)}, bf16[320,640]{1,0:T(8,128)(2,1)S(1)}, u32[]{:S(2)}, u32[]{:S(2)}) %collective-permute-start.4) | collective-permute-done | bytes 409632 | tf_op jit(solution)/shard_map/ppermute | solution.py:494
  37.9 5.0 %collective-permute-done.3.refs_1_ = bf16[320,640]{1,0:T(8,128)(2,1)S(1)} collective-permute-done((bf16[320,640]{1,0:T(8,128)(2,1)S(1)}, bf16[320,640]{1,0:T(8,128)(2,1)S(1)}, u32[]{:S(2)}, u32[]{:S(2)}) %collective-permute-start.3) | collective-permute-done | bytes 409632 | tf_op jit(solution)/shard_map/ppermute | solution.py:494
  43.0 0.2 shard_map.102
  43.1 0.9 %collective-permute-start.12 = (bf16[160,640]{1,0:T(8,128)(2,1)S(1)}, bf16[160,640]{1,0:T(8,128)(2,1)S(1)}, u32[]{:S(2)}, u32[]{:S(2)}) collective-permute-start(bf16[160,640]{1,0:T(8,128)(2,1)S(1)} %get-tuple-element.104), channel_id=1, source_target_pairs={{0,4},{4,0},{8,12},{12,8},{16,20},{20,16},{24,28},{28,24},{1,5},{5... | collective-permute-start | bytes 614408 | tf_op jit(solution)/shard_map/ppermute | solution.py:494
  44.0 0.0 collective-permute-start.13
  44.0 0.0 collective-permute-done.2.refs_1_
  44.0 0.4 shard_map.103
  44.5 4.0 %collective-permute-start.15 = (f32[8,384]{1,0:T(8,128)S(1)}, f32[8,384]{1,0:T(8,128)S(1)}, u32[]{:S(2)}, u32[]{:S(2)}) collective-permute-start(f32[8,384]{1,0:T(8,128)S(1)} %get-tuple-element.110.refs_0_), channel_id=1, source_target_pairs={{0,16},{4,20},{8,24},{12,28},{16,0},{20,4},{24,8},{28,12},{1,17},{... | collective-permute-start | bytes 36872 | tf_op jit(solution)/shard_map/ppermute | solution.py:494
  48.5 0.0 collective-permute-done.8.refs_1_
  48.5 0.0 collective-permute-done.9.refs_3_
  48.5 0.1 shard_map.105
  48.6 0.1 collective-permute-start.10
  48.7 0.9 %collective-permute-start.11 = (bf16[80,640]{1,0:T(8,128)(2,1)S(1)}, bf16[80,640]{1,0:T(8,128)(2,1)S(1)}, u32[]{:S(2)}, u32[]{:S(2)}) collective-permute-start(bf16[80,640]{1,0:T(8,128)(2,1)S(1)} %get-tuple-element.102), channel_id=1, source_target_pairs={{0,8},{4,12},{8,0},{12,4},{16,24},{20,28},{24,16},{28,20},{1,9},{5... | collective-permute-start | bytes 307208 | tf_op jit(solution)/shard_map/ppermute | solution.py:494
  49.6 0.9 %collective-permute-done.15.refs_1_ = f32[8,384]{1,0:T(8,128)S(1)} collective-permute-done((f32[8,384]{1,0:T(8,128)S(1)}, f32[8,384]{1,0:T(8,128)S(1)}, u32[]{:S(2)}, u32[]{:S(2)}) %collective-permute-start.15) | collective-permute-done | bytes 12320 | tf_op jit(solution)/shard_map/ppermute | solution.py:494
  50.6 0.5 collective-permute-start.16
  51.0 0.0 collective-permute-done.12.refs_1_
  51.0 2.2 %collective-permute-done.13.refs_3_ = bf16[160,640]{1,0:T(8,128)(2,1)S(1)} collective-permute-done((bf16[160,640]{1,0:T(8,128)(2,1)S(1)}, bf16[160,640]{1,0:T(8,128)(2,1)S(1)}, u32[]{:S(2)}, u32[]{:S(2)}) %collective-permute-start.13) | collective-permute-done | bytes 204832 | tf_op jit(solution)/shard_map/ppermute | solution.py:494
  53.2 0.1 shard_map.107
  53.3 1.3 %collective-permute-start.14 = (bf16[160,640]{1,0:T(8,128)(2,1)S(1)}, bf16[160,640]{1,0:T(8,128)(2,1)S(1)}, u32[]{:S(2)}, u32[]{:S(2)}) collective-permute-start(bf16[160,640]{1,0:T(8,128)(2,1)S(1)} %get-tuple-element.108), channel_id=1, source_target_pairs={{0,16},{4,20},{8,24},{12,28},{16,0},{20,4},{24,8},{28,12},{1,17},{... | collective-permute-start | bytes 614408 | tf_op jit(solution)/shard_map/ppermute | solution.py:494
  54.6 1.3 %collective-permute-start.7 = (bf16[320,128]{1,0:T(8,128)(2,1)S(1)}, bf16[320,128]{1,0:T(8,128)(2,1)S(1)}, u32[]{:S(2)}, u32[]{:S(2)}) collective-permute-start(bf16[320,128]{1,0:T(8,128)(2,1)S(1)} %get-tuple-element.94), channel_id=1, source_target_pairs={{4,0},{8,4},{12,8},{16,12},{20,16},{24,20},{28,24},{5,1},{9,5},{13... | collective-permute-start | bytes 245768 | tf_op jit(solution)/shard_map/ppermute | solution.py:499
  55.9 0.0 collective-permute-done.16.refs_1_
  55.9 3.1 %collective-permute-start.17 = (f32[8,384]{1,0:T(8,128)S(1)}, f32[8,384]{1,0:T(8,128)S(1)}, u32[]{:S(2)}, u32[]{:S(2)}) collective-permute-start(f32[8,384]{1,0:T(8,128)S(1)} %shard_map.109.refs_0_), channel_id=1, source_target_pairs={{0,8},{4,12},{8,0},{12,4},{16,24},{20,28},{24,16},{28,20},{1,9},{5... | collective-permute-start | bytes 36872 | tf_op jit(solution)/shard_map/ppermute | solution.py:494
  59.0 2.0 %collective-permute-done.10.refs_1_ = bf16[80,640]{1,0:T(8,128)(2,1)S(1)} collective-permute-done((bf16[80,640]{1,0:T(8,128)(2,1)S(1)}, bf16[80,640]{1,0:T(8,128)(2,1)S(1)}, u32[]{:S(2)}, u32[]{:S(2)}) %collective-permute-start.10) | collective-permute-done | bytes 102432 | tf_op jit(solution)/shard_map/ppermute | solution.py:494
  61.0 0.0 collective-permute-done.11.refs_3_
  61.0 0.8 %shard_map.106 = (f32[160,320]{1,0:T(8,128)}, f32[160,320]{1,0:T(8,128)S(1)}) custom-call(f32[80,640]{1,0:T(8,128)S(1)} %get-tuple-element.99.refs_0_.refs_4_.refs_2_, bf16[80,640]{1,0:T(8,128)(2,1)S(1)} %collective-permute-done.10.refs_1_, f32[80,640]{1,0:T(8,128)S(1)} %get-tuple-element.101.refs_2_, bf16[80,640]{1,0:T(8,128)(2,1)S(1)} %collective-permute-done.11.refs_3_), custom_call_target="tpu_custom_call" | custom-call | flops 30720000000 | bytes 3072000000 | tf_op jit(solution)/shard_map/pallas_call | solution.py:41
  61.8 0.0 collective-permute-done.7.came_ref
  61.8 0.9 %shard_map.104 = (bf16[320,384]{1,0:T(8,128)(2,1)}, f32[8,128]{1,0:T(8,128)S(1)}) custom-call(bf16[320,512]{1,0:T(8,128)(2,1)S(1)} %get-tuple-element.93.gx_ref, bf16[320,128]{1,0:T(8,128)(2,1)S(1)} %collective-permute-done.7.came_ref, s32[24,128]{1,0:T(8,128)S(1)} %bitcast.8), custom_call_target="tpu_custom_call" | custom-call | flops 6717440 | bytes 671744 | tf_op jit(solution)/shard_map/pallas_call | solution.py:41
  62.7 0.0 collective-permute-done.17.refs_1_
  62.7 0.0 copy-start.3
  62.7 1.5 %collective-permute-done.14.refs_2_ = bf16[160,640]{1,0:T(8,128)(2,1)S(1)} collective-permute-done((bf16[160,640]{1,0:T(8,128)(2,1)S(1)}, bf16[160,640]{1,0:T(8,128)(2,1)S(1)}, u32[]{:S(2)}, u32[]{:S(2)}) %collective-permute-start.14) | collective-permute-done | bytes 204832 | tf_op jit(solution)/shard_map/ppermute | solution.py:494
  64.2 1.0 %shard_map.111 = f32[3,160,320]{2,1,0:T(8,128)} custom-call(f32[160,320]{1,0:T(8,128)S(1)} %get-tuple-element.103.refs_0_, f32[160,640]{1,0:T(8,128)S(1)} %get-tuple-element.107.refs_2_.refs_1_, bf16[160,640]{1,0:T(8,128)(2,1)S(1)} %collective-permute-done.14.refs_2_, f32[8,128]{1,0:T(8,128)S(1)} %get-tuple-element.109.refs_2_.refs_3_, ...), custom_call_target="tpu_custom_call" | custom-call | flops 4300800000 | bytes 430080000 | tf_op jit(solution)/shard_map/pallas_call | solution.py:41
  65.2 0.0 copy-done.3
  (4 shorter events, 0.0 us)
Async XLA Ops:
  0.6 5.9 %copy-start.1 = (s32[3072]{0:T(1024)S(1)}, s32[3072]{0:T(1024)}, u32[]{:S(2)}) copy-start(s32[3072]{0:T(1024)} %param.11) | copy-start | bytes 36868
  1.7 12.6 %collective-permute-start = (bf16[128,1280]{1,0:T(8,128)(2,1)S(1)}, bf16[128,1280]{1,0:T(8,128)(2,1)S(1)}, u32[]{:S(2)}, u32[]{:S(2)}) collective-permute-start(bf16[128,1280]{1,0:T(8,128)(2,1)S(1)} %shard_map.93), channel_id=1, source_target_pairs={{0,4},{4,8},{8,12},{12,16},{16,20},{20,24},{24,28},{1,5},{5,9},{9,... | collective-permute-start | bytes 983048 | tf_op jit(solution)/shard_map/ppermute | solution.py:499
  6.5 7.7 %copy-start.2 = (f32[1280]{0:T(1024)S(1)}, f32[1280]{0:T(1024)}, u32[]{:S(2)}) copy-start(f32[1280]{0:T(1024)} %param.7) | copy-start | bytes 15364
  16.7 4.2 %copy-start = (bf16[384,1280]{1,0:T(8,128)(2,1)S(1)}, bf16[384,1280]{1,0:T(8,128)(2,1)}, u32[]{:S(2)}) copy-start(bf16[384,1280]{1,0:T(8,128)(2,1)} %refs_4_.1) | copy-start | bytes 2949124
  17.6 11.6 %collective-permute-start.6 = (bf16[320,640]{1,0:T(8,128)(2,1)S(1)}, bf16[320,640]{1,0:T(8,128)(2,1)S(1)}, u32[]{:S(2)}, u32[]{:S(2)}) collective-permute-start(bf16[320,640]{1,0:T(8,128)(2,1)S(1)} %get-tuple-element.90), channel_id=1, source_target_pairs={{0,4},{4,0},{8,12},{12,8},{16,20},{20,16},{24,28},{28,24},{1,5},{5... | collective-permute-start | bytes 1228808 | tf_op jit(solution)/shard_map/ppermute | solution.py:494
  19.3 11.5 %collective-permute-start.5 = (bf16[320,640]{1,0:T(8,128)(2,1)S(1)}, bf16[320,640]{1,0:T(8,128)(2,1)S(1)}, u32[]{:S(2)}, u32[]{:S(2)}) collective-permute-start(bf16[320,640]{1,0:T(8,128)(2,1)S(1)} %get-tuple-element.75.refs_6_), channel_id=1, source_target_pairs={{0,8},{4,12},{8,0},{12,4},{16,24},{20,28},{24,16},{28,20},{1,9},{5... | collective-permute-start | bytes 1228808 | tf_op jit(solution)/shard_map/ppermute | solution.py:494
  23.4 11.7 %collective-permute-start.1 = (bf16[2,336,512]{2,1,0:T(8,128)(2,1)S(1)}, bf16[2,336,512]{2,1,0:T(8,128)(2,1)S(1)}, u32[]{:S(2)}, u32[]{:S(2)}) collective-permute-start(bf16[2,336,512]{2,1,0:T(8,128)(2,1)S(1)} %get-tuple-element.77.refs_3_), channel_id=1, source_target_pairs={{0,1},{1,0},{2,3},{3,2},{4,5},{5,4},{6,7},{7,6},{8,9},{9,8},{10,11... | collective-permute-start | bytes 2064392 | tf_op jit(solution)/shard_map/ppermute | solution.py:494
  24.7 13.2 %collective-permute-start.4 = (bf16[320,640]{1,0:T(8,128)(2,1)S(1)}, bf16[320,640]{1,0:T(8,128)(2,1)S(1)}, u32[]{:S(2)}, u32[]{:S(2)}) collective-permute-start(bf16[320,640]{1,0:T(8,128)(2,1)S(1)} %get-tuple-element.87), channel_id=1, source_target_pairs={{0,4},{4,0},{8,12},{12,8},{16,20},{20,16},{24,28},{28,24},{1,5},{5... | collective-permute-start | bytes 1228808 | tf_op jit(solution)/shard_map/ppermute | solution.py:494
  26.2 16.7 %collective-permute-start.3 = (bf16[320,640]{1,0:T(8,128)(2,1)S(1)}, bf16[320,640]{1,0:T(8,128)(2,1)S(1)}, u32[]{:S(2)}, u32[]{:S(2)}) collective-permute-start(bf16[320,640]{1,0:T(8,128)(2,1)S(1)} %get-tuple-element.85.refs_6_), channel_id=1, source_target_pairs={{0,8},{4,12},{8,0},{12,4},{16,24},{20,28},{24,16},{28,20},{1,9},{5... | collective-permute-start | bytes 1228808 | tf_op jit(solution)/shard_map/ppermute | solution.py:494
  31.1 17.4 %collective-permute-start.8 = (bf16[160,640]{1,0:T(8,128)(2,1)S(1)}, bf16[160,640]{1,0:T(8,128)(2,1)S(1)}, u32[]{:S(2)}, u32[]{:S(2)}) collective-permute-start(bf16[160,640]{1,0:T(8,128)(2,1)S(1)} %get-tuple-element.96), channel_id=1, source_target_pairs={{0,4},{4,0},{8,12},{12,8},{16,20},{20,16},{24,28},{28,24},{1,5},{5... | collective-permute-start | bytes 614408 | tf_op jit(solution)/shard_map/ppermute | solution.py:494
  32.5 16.0 %collective-permute-start.9 = (bf16[160,640]{1,0:T(8,128)(2,1)S(1)}, bf16[160,640]{1,0:T(8,128)(2,1)S(1)}, u32[]{:S(2)}, u32[]{:S(2)}) collective-permute-start(bf16[160,640]{1,0:T(8,128)(2,1)S(1)} %get-tuple-element.98), channel_id=1, source_target_pairs={{0,16},{4,20},{8,24},{12,28},{16,0},{20,4},{24,8},{28,12},{1,17},{... | collective-permute-start | bytes 614408 | tf_op jit(solution)/shard_map/ppermute | solution.py:494
  35.3 8.8 %collective-permute-start.2 = (bf16[1,336,512]{2,1,0:T(8,128)(2,1)S(1)}, bf16[1,336,512]{2,1,0:T(8,128)(2,1)S(1)}, u32[]{:S(2)}, u32[]{:S(2)}) collective-permute-start(bf16[1,336,512]{2,1,0:T(8,128)(2,1)S(1)} %get-tuple-element.79), channel_id=1, source_target_pairs={{0,2},{1,3},{2,0},{3,1},{4,6},{5,7},{6,4},{7,5},{8,10},{9,11},{10,... | collective-permute-start | bytes 1032200 | tf_op jit(solution)/shard_map/ppermute | solution.py:494
  43.1 7.9 %collective-permute-start.12 = (bf16[160,640]{1,0:T(8,128)(2,1)S(1)}, bf16[160,640]{1,0:T(8,128)(2,1)S(1)}, u32[]{:S(2)}, u32[]{:S(2)}) collective-permute-start(bf16[160,640]{1,0:T(8,128)(2,1)S(1)} %get-tuple-element.104), channel_id=1, source_target_pairs={{0,4},{4,0},{8,12},{12,8},{16,20},{20,16},{24,28},{28,24},{1,5},{5... | collective-permute-start | bytes 614408 | tf_op jit(solution)/shard_map/ppermute | solution.py:494
  44.0 9.2 %collective-permute-start.13 = (bf16[160,640]{1,0:T(8,128)(2,1)S(1)}, bf16[160,640]{1,0:T(8,128)(2,1)S(1)}, u32[]{:S(2)}, u32[]{:S(2)}) collective-permute-start(bf16[160,640]{1,0:T(8,128)(2,1)S(1)} %get-tuple-element.106), channel_id=1, source_target_pairs={{0,8},{4,12},{8,0},{12,4},{16,24},{20,28},{24,16},{28,20},{1,9},{5... | collective-permute-start | bytes 614408 | tf_op jit(solution)/shard_map/ppermute | solution.py:494
  44.5 6.1 %collective-permute-start.15 = (f32[8,384]{1,0:T(8,128)S(1)}, f32[8,384]{1,0:T(8,128)S(1)}, u32[]{:S(2)}, u32[]{:S(2)}) collective-permute-start(f32[8,384]{1,0:T(8,128)S(1)} %get-tuple-element.110.refs_0_), channel_id=1, source_target_pairs={{0,16},{4,20},{8,24},{12,28},{16,0},{20,4},{24,8},{28,12},{1,17},{... | collective-permute-start | bytes 36872 | tf_op jit(solution)/shard_map/ppermute | solution.py:494
  48.6 12.4 %collective-permute-start.10 = (bf16[80,640]{1,0:T(8,128)(2,1)S(1)}, bf16[80,640]{1,0:T(8,128)(2,1)S(1)}, u32[]{:S(2)}, u32[]{:S(2)}) collective-permute-start(bf16[80,640]{1,0:T(8,128)(2,1)S(1)} %get-tuple-element.100), channel_id=1, source_target_pairs={{0,16},{4,20},{8,24},{12,28},{16,0},{20,4},{24,8},{28,12},{1,17},{... | collective-permute-start | bytes 307208 | tf_op jit(solution)/shard_map/ppermute | solution.py:494
  48.7 12.3 %collective-permute-start.11 = (bf16[80,640]{1,0:T(8,128)(2,1)S(1)}, bf16[80,640]{1,0:T(8,128)(2,1)S(1)}, u32[]{:S(2)}, u32[]{:S(2)}) collective-permute-start(bf16[80,640]{1,0:T(8,128)(2,1)S(1)} %get-tuple-element.102), channel_id=1, source_target_pairs={{0,8},{4,12},{8,0},{12,4},{16,24},{20,28},{24,16},{28,20},{1,9},{5... | collective-permute-start | bytes 307208 | tf_op jit(solution)/shard_map/ppermute | solution.py:494
  50.6 5.3 %collective-permute-start.16 = (f32[8,384]{1,0:T(8,128)S(1)}, f32[8,384]{1,0:T(8,128)S(1)}, u32[]{:S(2)}, u32[]{:S(2)}) collective-permute-start(f32[8,384]{1,0:T(8,128)S(1)} %shard_map.108.refs_0_), channel_id=1, source_target_pairs={{0,4},{4,0},{8,12},{12,8},{16,20},{20,16},{24,28},{28,24},{1,5},{5... | collective-permute-start | bytes 36872 | tf_op jit(solution)/shard_map/ppermute | solution.py:494
  53.3 10.9 %collective-permute-start.14 = (bf16[160,640]{1,0:T(8,128)(2,1)S(1)}, bf16[160,640]{1,0:T(8,128)(2,1)S(1)}, u32[]{:S(2)}, u32[]{:S(2)}) collective-permute-start(bf16[160,640]{1,0:T(8,128)(2,1)S(1)} %get-tuple-element.108), channel_id=1, source_target_pairs={{0,16},{4,20},{8,24},{12,28},{16,0},{20,4},{24,8},{28,12},{1,17},{... | collective-permute-start | bytes 614408 | tf_op jit(solution)/shard_map/ppermute | solution.py:494
  54.6 7.2 %collective-permute-start.7 = (bf16[320,128]{1,0:T(8,128)(2,1)S(1)}, bf16[320,128]{1,0:T(8,128)(2,1)S(1)}, u32[]{:S(2)}, u32[]{:S(2)}) collective-permute-start(bf16[320,128]{1,0:T(8,128)(2,1)S(1)} %get-tuple-element.94), channel_id=1, source_target_pairs={{4,0},{8,4},{12,8},{16,12},{20,16},{24,20},{28,24},{5,1},{9,5},{13... | collective-permute-start | bytes 245768 | tf_op jit(solution)/shard_map/ppermute | solution.py:499
  55.9 6.8 %collective-permute-start.17 = (f32[8,384]{1,0:T(8,128)S(1)}, f32[8,384]{1,0:T(8,128)S(1)}, u32[]{:S(2)}, u32[]{:S(2)}) collective-permute-start(f32[8,384]{1,0:T(8,128)S(1)} %shard_map.109.refs_0_), channel_id=1, source_target_pairs={{0,8},{4,12},{8,0},{12,4},{16,24},{20,28},{24,16},{28,20},{1,9},{5... | collective-permute-start | bytes 36872 | tf_op jit(solution)/shard_map/ppermute | solution.py:494
  62.7 2.5 %copy-start.3 = (f32[320]{0:T(512)}, f32[320]{0:T(512)S(1)}, u32[]{:S(2)}) copy-start(f32[320]{0:T(512)S(1)} %slice_reduce_fusion.refs_4_) | copy-start | bytes 3844

commit v3 on v2

--- a/solution.py
+++ b/solution.py
@@ -286,144 +286,167 @@
     return [[p + step * which for p in base] for which in (1 - mine, mine)]
 
 
-def gathered(own_ref, halo_ref, scratch, part, left, bits, sides=(0, 1)):
-    sub = part // len(bits)
-    to = 0
-    for chain, bit in enumerate(bits):
+def gathered(own_ref, halo_ref, scratch, part, left, cuts, sides=(0, 1)):
+    to = first = 0
+    for rows, bit in cuts:
         blocks = side_blocks(left, bit)
         for side in sides:
             for p in blocks[side]:
-                at = pl.ds(pl.multiple_of(p * part + chain * sub, 16), sub)
-                scratch[to : to + sub, :TILE] = halo_ref[at, :]
-                scratch[to : to + sub, TILE:] = own_ref[at, TILE:]
-                to += sub
-
-
-def out_query_product_kernel(part, left, bits, side, a_ref, a_halo_ref, b_ref, c_ref, c_halo_ref, d_ref, *refs):
+                at = pl.ds(pl.multiple_of(p * part + first, 16), rows)
+                scratch[to : to + rows, :TILE] = halo_ref[at, :]
+                scratch[to : to + rows, TILE:] = own_ref[at, TILE:]
+                to += rows
+        first += rows
+
+
+def row_spans(outs):
+    at = 0
+    for out in outs:
+        yield slice(at, at + out.shape[0]), out
+        at += out.shape[0]
+
+
+def out_query_product_kernel(
+    part, left, cuts, side, a_ref, a_halo_ref, b_ref, c_ref, c_halo_ref, d_ref, *refs
+):
     outs, (a_rows, c_rows) = refs[:-2], refs[-2:]
     share, rows = b_ref.shape
-    gathered(a_ref, a_halo_ref, a_rows, part, left, bits, (side,))
-    gathered(c_ref, c_halo_ref, c_rows, part, left, bits, (side,))
+    gathered(a_ref, a_halo_ref, a_rows, part, left, cuts, (side,))
+    gathered(c_ref, c_halo_ref, c_rows, part, left, cuts, (side,))
     gap = jnp.zeros((-share % TILE, rows), BF16)
     b = jnp.transpose(jnp.concatenate([b_ref[...], gap], axis=0))
     d = jnp.transpose(jnp.concatenate([gap, d_ref[...]], axis=0))
     shared = b.shape[1] - TILE
-    count = outs[0].shape[0]
-    for i, out in enumerate(outs):
-        at = slice(i * count, (i + 1) * count)
+    for at, out in row_spans(outs):
         one, two = dot(a_rows[at, :], b), dot(c_rows[at, :], d)
         out[:, :shared] = one[:, :shared].astype(out.dtype)
         out[:, shared : shared + TILE] = (one[:, shared:] + two[:, :TILE]).astype(out.dtype)
         out[:, shared + TILE :] = two[:, TILE:].astype(out.dtype)
 
 
-def pair_product_kernel(part, left, bits, a_ref, a_halo_ref, b_ref, *refs):
+def pair_product_kernel(part, left, cuts, a_ref, a_halo_ref, b_ref, *refs):
     outs, a_rows = refs[:-1], refs[-1]
     share, rows = b_ref.shape[1:]
-    gathered(a_ref, a_halo_ref, a_rows, part, left, bits)
+    gathered(a_ref, a_halo_ref, a_rows, part, left, cuts)
     b = jnp.transpose(b_ref[...].reshape(2 * share, rows))
-    count = outs[0].shape[0]
-    for i, out in enumerate(outs):
-        out[...] = dot(a_rows[i * count : (i + 1) * count, :], b).astype(out.dtype)
-
-
-def add_kernel(sub, lefts, bits, *refs):
-    chains = len(bits)
+    for at, out in row_spans(outs):
+        out[...] = dot(a_rows[at, :], b).astype(out.dtype)
+
+
+def add_kernel(lefts, cuts, *refs):
+    chains = len(cuts)
     ins, outs = refs[: 2 * chains], refs[2 * chains :]
     joined = len(outs) < 2 * chains
-    for chain, (left, bit) in enumerate(zip(lefts, bits)):
+    first = 0
+    for chain, (left, (rows, bit)) in enumerate(zip(lefts, cuts)):
         keep_ref, came_ref = ins[2 * chain : 2 * chain + 2]
-        first = chain if joined else 0
         for side, out in zip(side_blocks(left, bit), outs if joined else outs[2 * chain : 2 * chain + 2]):
             for i, p in enumerate(side):
-                at = pl.ds(pl.multiple_of(p * sub, 16), sub)
+                at = pl.ds(pl.multiple_of(p * rows, 16), rows)
                 total = keep_ref[at, :] + came_ref[at, :].astype(F32)
-                out[(first + i) * sub : (first + i + 1) * sub, :] = total.astype(out.dtype)
-
-
-def split_whole(total, sub, left, bit):
-    rows = lambda p: lax.dynamic_slice_in_dim(total, p * sub, sub, 0)
-    send, keep = [jnp.concatenate([rows(p) for p in side], axis=0) for side in side_blocks(left, bit)]
+                to = first + i * rows
+                out[to : to + rows, :] = total.astype(out.dtype)
+        first += rows if joined else 0
+
+
+def split_whole(total, rows, left, bit):
+    block = lambda p: lax.dynamic_slice_in_dim(total, p * rows, rows, 0)
+    send, keep = [jnp.concatenate([block(p) for p in side], axis=0) for side in side_blocks(left, bit)]
     return [send.astype(BF16), keep]
 
 
-def split_product(product, part, left, bits):
-    sub = part // len(bits)
-    by_chain = product.reshape(-1, len(bits), sub, product.shape[1])
+def split_product(product, part, left, cuts):
+    blocks = product.reshape(-1, part, product.shape[1])
     out = []
-    for chain, bit in enumerate(bits):
-        out += split_whole(by_chain[:, chain].reshape(-1, product.shape[1]), sub, left, bit)
+    first = 0
+    for rows, bit in cuts:
+        mine = blocks[:, first : first + rows].reshape(-1, product.shape[1])
+        out += split_whole(mine, rows, left, bit)
+        first += rows
     return out
 
 
-def halves(rows, width, chains):
-    return [shape((rows // 2, width)), shape((rows // 2, width), F32)] * chains
-
-
-def out_query_product(part, left, bits, a, a_halo, b, c, c_halo, d, side, after=()):
+def whole_tiles(cuts):
+    return all(rows % 16 == 0 for rows, _ in cuts)
+
+
+def halves(blocks, width, cuts):
+    out = []
+    for rows, _ in cuts:
+        out += [shape((blocks // 2 * rows, width)), shape((blocks // 2 * rows, width), F32)]
+    return out
+
+
+def out_query_product(part, left, cuts, a, a_halo, b, c, c_halo, d, side, after=()):
     features = a.shape[0]
     share, rows = b.shape
-    if part % (16 * len(bits)):
+    if not whole_tiles(cuts):
         a = jnp.concatenate([a_halo, a[:, TILE:]], axis=1)
         c = jnp.concatenate([c_halo, c[:, TILE:]], axis=1)
         product = jnp.concatenate([dot(a, b, NT), dot(c, d, NT)], axis=1)
-        return split_product(product, part, left, bits)[side::2]
+        return split_product(product, part, left, cuts)[side::2]
     return call(
-        functools.partial(out_query_product_kernel, part, left, bits, side),
-        halves(features // len(bits), 2 * share, len(bits))[side::2],
+        functools.partial(out_query_product_kernel, part, left, cuts, side),
+        halves(features // part, 2 * share, cuts)[side::2],
         a, a_halo, b, c, c_halo, d, after=after, weight=1,
         scratch_shapes=[pltpu.VMEM((features // 2, rows), BF16)] * 2,
     )
 
 
-def pair_product(part, left, bits, a, a_halo, b, after):
+def pair_product(part, left, cuts, a, a_halo, b, after):
     features = a.shape[0]
     _, share, rows = b.shape
-    if part % (16 * len(bits)):
+    if not whole_tiles(cuts):
         a = jnp.concatenate([a_halo, a[:, TILE:]], axis=1)
-        return split_product(dot(a, b.reshape(2 * share, rows), NT), part, left, bits)
+        return split_product(dot(a, b.reshape(2 * share, rows), NT), part, left, cuts)
     return call(
-        functools.partial(pair_product_kernel, part, left, bits),
-        halves(features // len(bits), 2 * share, len(bits)), a, a_halo, b, after=after,
+        functools.partial(pair_product_kernel, part, left, cuts),
+        halves(features // part, 2 * share, cuts), a, a_halo, b, after=after,
         scratch_shapes=[pltpu.VMEM((features, rows), BF16)],
     )
 
 
-def add_split(sub, lefts, bits, pairs, after, weight):
-    joined = len(lefts[0]) == 1 and len(set(bits)) == 1
-    if sub % 16:
-        parts = sum(
-            [split_whole(k + c.astype(F32), sub, l, b) for (k, c), l, b in zip(pairs, lefts, bits)], []
-        )
+def add_split(lefts, cuts, pairs, after, weight):
+    joined = len(lefts[0]) == 1 and len({bit for _, bit in cuts}) == 1
+    if not whole_tiles(cuts):
+        parts = []
+        for (keep, came), left, (rows, bit) in zip(pairs, lefts, cuts):
+            parts += split_whole(keep + came.astype(F32), rows, left, bit)
         return [jnp.concatenate(parts[i::2], axis=0) for i in range(2)] if joined else parts
-    outs = halves(*pairs[0][0].shape, len(bits))
+    width = pairs[0][0].shape[1]
+    outs = halves(1 << len(lefts[0]), width, cuts)
     if joined:
-        outs = [shape((len(bits) * sub, o.shape[1]), o.dtype) for o in outs[:2]]
+        rows = sum(rows for rows, _ in cuts)
+        outs = [shape((rows, width)), shape((rows, width), F32)]
     return call(
-        functools.partial(add_kernel, sub, lefts, bits), outs, *[t for pair in pairs for t in pair],
+        functools.partial(add_kernel, lefts, cuts), outs, *[t for pair in pairs for t in pair],
         after=after, weight=weight,
     )
+
+
+def summed(ins):
+    at = 0
+    for keep, came in zip(ins[::2], ins[1::2]):
+        rows = keep.shape[0]
+        yield slice(at, at + rows), keep[...] + came[...].astype(F32)
+        at += rows
 
 
 def finish_out_query_kernel(*refs):
     ins, (out_ref, query_ref) = refs[:-2], refs[-2:]
-    sub, width = ins[0].shape
-    for chain in range(len(ins) // 2):
-        total = ins[2 * chain][...] + ins[2 * chain + 1][...].astype(F32)
-        rows = slice(chain * sub, (chain + 1) * sub)
-        out_ref[rows, :] = total[:, : width // 2]
-        query_ref[rows, :] = total[:, width // 2 :]
+    share = out_ref.shape[1]
+    for rows, total in summed(ins):
+        out_ref[rows, :] = total[:, :share]
+        query_ref[rows, :] = total[:, share:]
 
 
 def finish_kernel(query_ref, *refs):
     ins, qkv_ref = refs[:-1], refs[-1]
-    sub, width = ins[0].shape
+    share = qkv_ref.shape[2]
     qkv_ref[0] = query_ref[...]
-    for chain in range(len(ins) // 2):
-        total = ins[2 * chain][...] + ins[2 * chain + 1][...].astype(F32)
-        rows = slice(chain * sub, (chain + 1) * sub)
-        qkv_ref[1, rows, :] = total[:, : width // 2]
-        qkv_ref[2, rows, :] = total[:, width // 2 :]
+    for rows, total in summed(ins):
+        qkv_ref[1, rows, :] = total[:, :share]
+        qkv_ref[2, rows, :] = total[:, share:]
 
 
 def normed_grad_kernel(gq_ref, gkv_ref, w_ref, gain_ref, x_ref, halo_ref, send_ref, keep_ref):
@@ -555,21 +578,26 @@
         orders_first = [[1, 0, 2] + rest, [0, 2, 1] + rest]
         orders_second = [[1, 0, 2] + rest, [0, 1, 2] + rest]
     every = list(range(levels - 1, -1, -1))
-    sub = part // len(orders_first)
-    bits = lambda orders, step: [order[step] for order in orders]
+    def sizes(orders):
+        if len(orders) == 1:
+            return [part]
+        short = part // 2 if part % 32 or orders is orders_first else part * 2 // 5 // 16 * 16
+        return [short, part - short]
+
+    cuts = lambda orders, step: [(rows, order[step]) for rows, order in zip(sizes(orders), orders)]
 
     def exchange(parts, orders, step):
         return [
             (keep, swap(send, "vis", 1 << bit))
-            for send, keep, bit in zip(parts[::2], parts[1::2], bits(orders, step))
+            for send, keep, (_, bit) in zip(parts[::2], parts[1::2], cuts(orders, step))
         ]
 
     def add(pairs, orders, step, weight, after=()):
         lefts = [[b for b in every if b not in order[:step]] for order in orders]
-        return exchange(add_split(sub, lefts, bits(orders, step), pairs, after, weight), orders, step)
+        return exchange(add_split(lefts, cuts(orders, step), pairs, after, weight), orders, step)
 
     first_product = functools.partial(
-        out_query_product, part, every, bits(orders_first, 0),
+        out_query_product, part, every, cuts(orders_first, 0),
         grad_y_t, grad_y_halo, attended, normed, normed_halo, grad_q,
     )
     sends = first_product(0)
@@ -579,7 +607,7 @@
         grad_q, grad_kv, w_here, gain, patches, edge, after=sends[:1],
     )
     parts = pair_product(
-        part, every, bits(orders_second, 0), normed, normed_halo, grad_kv, (send,)
+        part, every, cuts(orders_second, 0), normed, normed_halo, grad_kv, (send,)
     )
     keeps = first_product(1, parts[:1])
     first = exchange([t for pair in zip(sends, keeps) for t in pair], orders_first, 0)
@@ -609,11 +637,11 @@
         merge_kernel, [shape((share, rows)), shape((8, TILE), F32)],
         grad_x, shift(grad_x_halo, "vis", -1), ids, weight=1,
     )
-    for i, bit in enumerate(sorted(range(levels), key=lambda bit: (bit != 2, bit))):
+    for bit in range(levels):
         came = swap(grad_gain, "vis", 1 << bit)
         (grad_gain,) = call(
             gain_add_kernel, [shape(grad_gain.shape, F32)], grad_gain, came,
-            weight=1, after=(*next(tokens, ()), *((token,) if i == 2 else ())),
+            weight=1, after=(*next(tokens, ()), *((token,) if bit == 2 else ())),
         )
     grad_gain = grad_gain[0, :share]
     flat = lambda pairs: [t for pair in pairs for t in pair]

time: 65.4 us -> 65.3 us (level)
  waiting for transfers between devices: 16.5 us -> 12.2 us
  starting transfers between devices: 27.3 us -> 31.5 us
    ppermute x16, waiting for transfers between devices: 16.5 us -> 12.2 us  [swap(): return lax.ppermute(block, axis, [(i, i ^ distance) for i in devices])]
    ppermute x16, starting transfers between devices: 21.2 us -> 25.4 us  [swap(): return lax.ppermute(block, axis, [(i, i ^ distance) for i in devices])]
  transfers between devices with their start and end apart: 18 -> 18, of which waited for: 8 -> 5; matrix products, arithmetic and copies ran while one was open for 0% -> 0% of each run, Pallas kernels for 23% -> 23%
where the time goes in v3:
time: 65.3 us; the launch traced here: 65.1 us
  starting transfers between devices  31.5 us (48%)
  Pallas kernels  20.5 us (31%)
  waiting for transfers between devices  12.2 us (19%)
  between operations  0.82 us (1%)
    ppermute x16, starting transfers between devices, swap(): return lax.ppermute(block, axis, [(i, i ^ distance) for i in devices])  25.4 us
    pallas_call x19, Pallas kernels, call(): pl.pallas_call(kernel, in_specs=specs, out_shape=outs, compiler_params=pl...  20.5 us
    ppermute x16, waiting for transfers between devices, swap(): return lax.ppermute(block, axis, [(i, i ^ distance) for i in devices])  12.2 us
    ppermute x2, starting transfers between devices, shift(): lax.ppermute(block, axis, [(i, i + by) for i in range(count) if 0 <= i +...  6.14 us
  transfers between devices with their start and end apart: 18, of which 5 were waited for; matrix products, arithmetic and copies ran while one was open for 0% of the time, Pallas kernels for 23%

profile of v3, /device:TPU:0, one launch (start us, length us, event | category | flops | bytes accessed | tf_op | source)
XLA Modules:
  0.0 65.1 jit_solution(15092864508086182698)
XLA Ops:
  0.6 0.0 copy-start.1
  0.6 1.0 %shard_map.93 = bf16[128,1280]{1,0:T(8,128)(2,1)S(1)} custom-call(bf16[384,1280]{1,0:T(8,128)(2,1)} %refs_4_.1, bf16[384,1280]{1,0:T(8,128)(2,1)} %gy_any.3), custom_call_target="tpu_custom_call" | custom-call | flops 22937600 | bytes 2293760 | tf_op jit(solution)/shard_map/pallas_call | solution.py:41
  1.7 4.9 %collective-permute-start = (bf16[128,1280]{1,0:T(8,128)(2,1)S(1)}, bf16[128,1280]{1,0:T(8,128)(2,1)S(1)}, u32[]{:S(2)}, u32[]{:S(2)}) collective-permute-start(bf16[128,1280]{1,0:T(8,128)(2,1)S(1)} %shard_map.93), channel_id=1, source_target_pairs={{0,4},{4,8},{8,12},{12,16},{16,20},{20,24},{24,28},{1,5},{5,9},{9,... | collective-permute-start | bytes 983048 | tf_op jit(solution)/shard_map/ppermute | solution.py:522
  6.5 0.0 copy-done.1
  6.5 0.0 copy-start.2
  6.6 7.7 %shard_map.94 = (bf16[1280,512]{1,0:T(8,128)(2,1)S(1)}, bf16[1280,512]{1,0:T(8,128)(2,1)S(1)}, f32[8,512]{1,0:T(8,128)S(1)}, bf16[320,512]{1,0:T(8,128)(2,1)S(1)...) custom-call(bf16[384,1280]{1,0:T(8,128)(2,1)} %refs_4_.1, ...), custom_call_target="tpu_custom_call" | custom-call | flops 149432320 | bytes 14943232 | tf_op jit(solution)/shard_map/pallas_call | solution.py:41
  14.2 0.0 collective-permute-done.edge_ref.refs_5_
  14.3 0.0 copy-done.2
  14.3 2.4 %shard_map.95 = (bf16[320,512]{1,0:T(8,128)(2,1)S(1)}, bf16[320,512]{1,0:T(8,128)(2,1)S(1)}, bf16[2,320,512]{2,1,0:T(8,128)(2,1)S(1)}, bf16[1280,128]{1,0:T(8,12...) custom-call(bf16[128,1280]{1,0:T(8,128)(2,1)S(1)} %collective-permut, ...), custom_call_target="tpu_custom_call" | custom-call | flops 98805760 | bytes 9880576 | tf_op jit(solution)/shard_map/pallas_call | solution.py:41
  16.7 0.0 copy-start
  16.7 0.9 %shard_map.96 = (bf16[320,640]{1,0:T(8,128)(2,1)S(1)}, bf16[320,640]{1,0:T(8,128)(2,1)S(1)}) custom-call(bf16[1280,512]{1,0:T(8,128)(2,1)S(1)} %get-tuple-element.70.a_ref.refs_0_, bf16[1280,128]{1,0:T(8,128)(2,1)S(1)} %get-tuple-element.71.a_halo_ref.refs_1_, bf16[320,512]{1,0:T(8,128)(2,1)S(1)} %get-tuple-element.72.b_ref.refs_2_, ...), custom_call_target="tpu_custom_call" | custom-call | flops 47513600 | bytes 4751360 | tf_op jit(solution)/shard_map/pallas_call | solution.py:41
  17.6 1.7 %collective-permute-start.6 = (bf16[320,640]{1,0:T(8,128)(2,1)S(1)}, bf16[320,640]{1,0:T(8,128)(2,1)S(1)}, u32[]{:S(2)}, u32[]{:S(2)}) collective-permute-start(bf16[320,640]{1,0:T(8,128)(2,1)S(1)} %get-tuple-element.90), channel_id=1, source_target_pairs={{0,4},{4,0},{8,12},{12,8},{16,20},{20,16},{24,28},{28,24},{1,5},{5... | collective-permute-start | bytes 1228808 | tf_op jit(solution)/shard_map/ppermute | solution.py:517
  19.3 1.6 %collective-permute-start.5 = (bf16[320,640]{1,0:T(8,128)(2,1)S(1)}, bf16[320,640]{1,0:T(8,128)(2,1)S(1)}, u32[]{:S(2)}, u32[]{:S(2)}) collective-permute-start(bf16[320,640]{1,0:T(8,128)(2,1)S(1)} %get-tuple-element.75.refs_6_), channel_id=1, source_target_pairs={{0,8},{4,12},{8,0},{12,4},{16,24},{20,28},{24,16},{28,20},{1,9},{5... | collective-permute-start | bytes 1228808 | tf_op jit(solution)/shard_map/ppermute | solution.py:517
  20.9 0.0 copy-done
  20.9 2.5 %shard_map.97 = (bf16[2,336,512]{2,1,0:T(8,128)(2,1)S(1)}, bf16[2,336,512]{2,1,0:T(8,128)(2,1)S(1)}) custom-call(bf16[320,512]{1,0:T(8,128)(2,1)S(1)} %get-tuple-element.68.d_ref.refs_0_.refs_5_, bf16[2,320,512]{2,1,0:T(8,128)(2,1)S(1)} %get-tuple-element.69.refs_1_.refs_2_, bf16[3,320,1280]{2,1,0:T(8,128)(2,1)S(1)} %get-tuple-element.59.w_ref.refs_2_, ...), custom_call_target="tpu_custom_call" | custom-call | flops 18398208000 | bytes 1839820800 | tf_op jit(solution)/shard_map/pallas_call | solution.py:41
  23.4 0.1 collective-permute-start.1
  23.5 1.3 %shard_map.99 = (bf16[256,640]{1,0:T(8,128)(2,1)S(1)}, f32[256,640]{1,0:T(8,128)S(1)}, bf16[384,640]{1,0:T(8,128)(2,1)S(1)}, f32[384,640]{1,0:T(8,128)S(1)}) custom-call(bf16[1280,512]{1,0:T(8,128)(2,1)S(1)} %get-tuple-element.73.c_ref.refs_0_.refs_3_, bf16[1280,128]{1,0:T(8,128)(2,1)S(1)} %get-tuple-element.74.c_halo_ref.refs_1_.refs_4_, ...), custom_call_target="tpu_custom_call" | custom-call | flops 14254080000 | bytes 1425408000 | tf_op jit(solution)/shard_map/pallas_call | solution.py:41
  24.7 0.5 collective-permute-start.3
  25.3 1.1 %collective-permute-start.4 = (bf16[384,640]{1,0:T(8,128)(2,1)S(1)}, bf16[384,640]{1,0:T(8,128)(2,1)S(1)}, u32[]{:S(2)}, u32[]{:S(2)}) collective-permute-start(bf16[384,640]{1,0:T(8,128)(2,1)S(1)} %get-tuple-element.87), channel_id=1, source_target_pairs={{0,4},{4,0},{8,12},{12,8},{16,20},{20,16},{24,28},{28,24},{1,5},{5... | collective-permute-start | bytes 1474568 | tf_op jit(solution)/shard_map/ppermute | solution.py:517
  26.3 0.9 %shard_map.100 = (f32[320,640]{1,0:T(8,128)S(1)}, f32[320,640]{1,0:T(8,128)S(1)}) custom-call(bf16[1280,512]{1,0:T(8,128)(2,1)S(1)} %get-tuple-element.70.a_ref.refs_0_, bf16[1280,128]{1,0:T(8,128)(2,1)S(1)} %get-tuple-element.71.a_halo_ref.refs_1_, bf16[320,512]{1,0:T(8,128)(2,1)S(1)} %get-tuple-element.72.b_ref.refs_2_, ...), custom_call_target="tpu_custom_call" | custom-call | flops 55705600 | bytes 5570560 | tf_op jit(solution)/shard_map/pallas_call | solution.py:41
  27.2 1.8 %collective-permute-done.6.refs_3_ = bf16[320,640]{1,0:T(8,128)(2,1)S(1)} collective-permute-done((bf16[320,640]{1,0:T(8,128)(2,1)S(1)}, bf16[320,640]{1,0:T(8,128)(2,1)S(1)}, u32[]{:S(2)}, u32[]{:S(2)}) %collective-permute-start.6) | collective-permute-done | bytes 409632 | tf_op jit(solution)/shard_map/ppermute | solution.py:517
  29.0 2.7 %collective-permute-done.5.refs_1_ = bf16[320,640]{1,0:T(8,128)(2,1)S(1)} collective-permute-done((bf16[320,640]{1,0:T(8,128)(2,1)S(1)}, bf16[320,640]{1,0:T(8,128)(2,1)S(1)}, u32[]{:S(2)}, u32[]{:S(2)}) %collective-permute-start.5) | collective-permute-done | bytes 409632 | tf_op jit(solution)/shard_map/ppermute | solution.py:517
  31.7 0.3 shard_map.101
  32.0 0.6 collective-permute-start.8
  32.7 2.6 %collective-permute-start.9 = (bf16[160,640]{1,0:T(8,128)(2,1)S(1)}, bf16[160,640]{1,0:T(8,128)(2,1)S(1)}, u32[]{:S(2)}, u32[]{:S(2)}) collective-permute-start(bf16[160,640]{1,0:T(8,128)(2,1)S(1)} %get-tuple-element.98), channel_id=1, source_target_pairs={{0,16},{4,20},{8,24},{12,28},{16,0},{20,4},{24,8},{28,12},{1,17},{... | collective-permute-start | bytes 614408 | tf_op jit(solution)/shard_map/ppermute | solution.py:517
  35.2 0.0 collective-permute-done.1.came_ref
  35.2 0.1 shard_map.98
  35.4 1.6 %collective-permute-start.2 = (bf16[1,336,512]{2,1,0:T(8,128)(2,1)S(1)}, bf16[1,336,512]{2,1,0:T(8,128)(2,1)S(1)}, u32[]{:S(2)}, u32[]{:S(2)}) collective-permute-start(bf16[1,336,512]{2,1,0:T(8,128)(2,1)S(1)} %get-tuple-element.79), channel_id=1, source_target_pairs={{0,2},{1,3},{2,0},{3,1},{4,6},{5,7},{6,4},{7,5},{8,10},{9,11},{10,... | collective-permute-start | bytes 1032200 | tf_op jit(solution)/shard_map/ppermute | solution.py:517
  37.0 3.9 %collective-permute-done.3.refs_1_ = bf16[256,640]{1,0:T(8,128)(2,1)S(1)} collective-permute-done((bf16[256,640]{1,0:T(8,128)(2,1)S(1)}, bf16[256,640]{1,0:T(8,128)(2,1)S(1)}, u32[]{:S(2)}, u32[]{:S(2)}) %collective-permute-start.3) | collective-permute-done | bytes 327712 | tf_op jit(solution)/shard_map/ppermute | solution.py:517
  40.9 0.0 collective-permute-done.4.refs_3_
  40.9 0.1 shard_map.102
  41.0 0.4 collective-permute-start.12
  41.4 1.5 %collective-permute-start.13 = (bf16[192,640]{1,0:T(8,128)(2,1)S(1)}, bf16[192,640]{1,0:T(8,128)(2,1)S(1)}, u32[]{:S(2)}, u32[]{:S(2)}) collective-permute-start(bf16[192,640]{1,0:T(8,128)(2,1)S(1)} %get-tuple-element.106), channel_id=1, source_target_pairs={{0,8},{4,12},{8,0},{12,4},{16,24},{20,28},{24,16},{28,20},{1,9},{5... | collective-permute-start | bytes 737288 | tf_op jit(solution)/shard_map/ppermute | solution.py:517
  42.9 0.0 collective-permute-done.2.refs_1_
  42.9 0.4 shard_map.103
  43.4 1.4 %collective-permute-start.15 = (f32[8,384]{1,0:T(8,128)S(1)}, f32[8,384]{1,0:T(8,128)S(1)}, u32[]{:S(2)}, u32[]{:S(2)}) collective-permute-start(f32[8,384]{1,0:T(8,128)S(1)} %get-tuple-element.110.refs_0_), channel_id=1, source_target_pairs={{0,4},{4,0},{8,12},{12,8},{16,20},{20,16},{24,28},{28,24},{1,5},{5... | collective-permute-start | bytes 36872 | tf_op jit(solution)/shard_map/ppermute | solution.py:517
  44.8 0.0 collective-permute-done.8.refs_1_
  44.8 0.0 collective-permute-done.9.refs_3_
  44.8 0.1 shard_map.105
  44.9 2.7 %collective-permute-start.10 = (bf16[80,640]{1,0:T(8,128)(2,1)S(1)}, bf16[80,640]{1,0:T(8,128)(2,1)S(1)}, u32[]{:S(2)}, u32[]{:S(2)}) collective-permute-start(bf16[80,640]{1,0:T(8,128)(2,1)S(1)} %get-tuple-element.100), channel_id=1, source_target_pairs={{0,16},{4,20},{8,24},{12,28},{16,0},{20,4},{24,8},{28,12},{1,17},{... | collective-permute-start | bytes 307208 | tf_op jit(solution)/shard_map/ppermute | solution.py:517
  47.6 1.6 %collective-permute-start.11 = (bf16[80,640]{1,0:T(8,128)(2,1)S(1)}, bf16[80,640]{1,0:T(8,128)(2,1)S(1)}, u32[]{:S(2)}, u32[]{:S(2)}) collective-permute-start(bf16[80,640]{1,0:T(8,128)(2,1)S(1)} %get-tuple-element.102), channel_id=1, source_target_pairs={{0,8},{4,12},{8,0},{12,4},{16,24},{20,28},{24,16},{28,20},{1,9},{5... | collective-permute-start | bytes 307208 | tf_op jit(solution)/shard_map/ppermute | solution.py:517
  49.2 0.0 collective-permute-done.15.refs_1_
  49.2 0.4 collective-permute-start.16
  49.7 0.0 collective-permute-done.12.refs_1_
  49.7 1.7 %collective-permute-done.13.refs_3_ = bf16[192,640]{1,0:T(8,128)(2,1)S(1)} collective-permute-done((bf16[192,640]{1,0:T(8,128)(2,1)S(1)}, bf16[192,640]{1,0:T(8,128)(2,1)S(1)}, u32[]{:S(2)}, u32[]{:S(2)}) %collective-permute-start.13) | collective-permute-done | bytes 245792 | tf_op jit(solution)/shard_map/ppermute | solution.py:517
  51.4 0.1 shard_map.107
  51.5 1.7 %collective-permute-start.14 = (bf16[160,640]{1,0:T(8,128)(2,1)S(1)}, bf16[160,640]{1,0:T(8,128)(2,1)S(1)}, u32[]{:S(2)}, u32[]{:S(2)}) collective-permute-start(bf16[160,640]{1,0:T(8,128)(2,1)S(1)} %get-tuple-element.108), channel_id=1, source_target_pairs={{0,16},{4,20},{8,24},{12,28},{16,0},{20,4},{24,8},{28,12},{1,17},{... | collective-permute-start | bytes 614408 | tf_op jit(solution)/shard_map/ppermute | solution.py:517
  53.1 1.3 %collective-permute-start.7 = (bf16[320,128]{1,0:T(8,128)(2,1)S(1)}, bf16[320,128]{1,0:T(8,128)(2,1)S(1)}, u32[]{:S(2)}, u32[]{:S(2)}) collective-permute-start(bf16[320,128]{1,0:T(8,128)(2,1)S(1)} %get-tuple-element.94), channel_id=1, source_target_pairs={{4,0},{8,4},{12,8},{16,12},{20,16},{24,20},{28,24},{5,1},{9,5},{13... | collective-permute-start | bytes 245768 | tf_op jit(solution)/shard_map/ppermute | solution.py:522
  54.4 0.0 collective-permute-done.16.refs_1_
  54.4 5.9 %collective-permute-start.17 = (f32[8,384]{1,0:T(8,128)S(1)}, f32[8,384]{1,0:T(8,128)S(1)}, u32[]{:S(2)}, u32[]{:S(2)}) collective-permute-start(f32[8,384]{1,0:T(8,128)S(1)} %shard_map.109.refs_0_), channel_id=1, source_target_pairs={{0,16},{4,20},{8,24},{12,28},{16,0},{20,4},{24,8},{28,12},{1,17},{... | collective-permute-start | bytes 36872 | tf_op jit(solution)/shard_map/ppermute | solution.py:517
  60.3 0.0 collective-permute-done.10.refs_1_
  60.3 0.0 collective-permute-done.11.refs_3_
  60.3 0.8 %shard_map.106 = (f32[160,320]{1,0:T(8,128)}, f32[160,320]{1,0:T(8,128)S(1)}) custom-call(f32[80,640]{1,0:T(8,128)S(1)} %get-tuple-element.99.refs_0_.refs_4_.refs_2_, bf16[80,640]{1,0:T(8,128)(2,1)S(1)} %collective-permute-done.10.refs_1_, f32[80,640]{1,0:T(8,128)S(1)} %get-tuple-element.101.refs_2_, bf16[80,640]{1,0:T(8,128)(2,1)S(1)} %collective-permute-done.11.refs_3_), custom_call_target="tpu_custom_call" | custom-call | flops 30720000000 | bytes 3072000000 | tf_op jit(solution)/shard_map/pallas_call | solution.py:41
  61.1 0.0 collective-permute-done.7.came_ref
  61.1 0.9 %shard_map.104 = (bf16[320,384]{1,0:T(8,128)(2,1)}, f32[8,128]{1,0:T(8,128)S(1)}) custom-call(bf16[320,512]{1,0:T(8,128)(2,1)S(1)} %get-tuple-element.93.gx_ref, bf16[320,128]{1,0:T(8,128)(2,1)S(1)} %collective-permute-done.7.came_ref, s32[24,128]{1,0:T(8,128)S(1)} %bitcast.8), custom_call_target="tpu_custom_call" | custom-call | flops 6717440 | bytes 671744 | tf_op jit(solution)/shard_map/pallas_call | solution.py:41
  62.0 2.1 %collective-permute-done.17.refs_1_ = f32[8,384]{1,0:T(8,128)S(1)} collective-permute-done((f32[8,384]{1,0:T(8,128)S(1)}, f32[8,384]{1,0:T(8,128)S(1)}, u32[]{:S(2)}, u32[]{:S(2)}) %collective-permute-start.17) | collective-permute-done | bytes 12320 | tf_op jit(solution)/shard_map/ppermute | solution.py:517
  64.1 0.0 copy-start.3
  64.1 0.0 collective-permute-done.14.refs_2_
  64.1 1.0 %shard_map.111 = f32[3,160,320]{2,1,0:T(8,128)} custom-call(f32[160,320]{1,0:T(8,128)S(1)} %get-tuple-element.103.refs_0_, f32[160,640]{1,0:T(8,128)S(1)} %get-tuple-element.107.refs_2_.refs_1_, bf16[160,640]{1,0:T(8,128)(2,1)S(1)} %collective-permute-done.14.refs_2_, f32[8,128]{1,0:T(8,128)S(1)} %get-tuple-element.109.refs_2_.refs_3_, ...), custom_call_target="tpu_custom_call" | custom-call | flops 4300800000 | bytes 430080000 | tf_op jit(solution)/shard_map/pallas_call | solution.py:41
  65.1 0.0 copy-done.3
  (4 shorter events, 0.0 us)
Async XLA Ops:
  0.6 5.9 %copy-start.1 = (s32[3072]{0:T(1024)S(1)}, s32[3072]{0:T(1024)}, u32[]{:S(2)}) copy-start(s32[3072]{0:T(1024)} %param.11) | copy-start | bytes 36868
  1.7 12.6 %collective-permute-start = (bf16[128,1280]{1,0:T(8,128)(2,1)S(1)}, bf16[128,1280]{1,0:T(8,128)(2,1)S(1)}, u32[]{:S(2)}, u32[]{:S(2)}) collective-permute-start(bf16[128,1280]{1,0:T(8,128)(2,1)S(1)} %shard_map.93), channel_id=1, source_target_pairs={{0,4},{4,8},{8,12},{12,16},{16,20},{20,24},{24,28},{1,5},{5,9},{9,... | collective-permute-start | bytes 983048 | tf_op jit(solution)/shard_map/ppermute | solution.py:522
  6.5 7.7 %copy-start.2 = (f32[1280]{0:T(1024)S(1)}, f32[1280]{0:T(1024)}, u32[]{:S(2)}) copy-start(f32[1280]{0:T(1024)} %param.7) | copy-start | bytes 15364
  16.7 4.2 %copy-start = (bf16[384,1280]{1,0:T(8,128)(2,1)S(1)}, bf16[384,1280]{1,0:T(8,128)(2,1)}, u32[]{:S(2)}) copy-start(bf16[384,1280]{1,0:T(8,128)(2,1)} %refs_4_.1) | copy-start | bytes 2949124
  17.6 11.4 %collective-permute-start.6 = (bf16[320,640]{1,0:T(8,128)(2,1)S(1)}, bf16[320,640]{1,0:T(8,128)(2,1)S(1)}, u32[]{:S(2)}, u32[]{:S(2)}) collective-permute-start(bf16[320,640]{1,0:T(8,128)(2,1)S(1)} %get-tuple-element.90), channel_id=1, source_target_pairs={{0,4},{4,0},{8,12},{12,8},{16,20},{20,16},{24,28},{28,24},{1,5},{5... | collective-permute-start | bytes 1228808 | tf_op jit(solution)/shard_map/ppermute | solution.py:517
  19.3 12.4 %collective-permute-start.5 = (bf16[320,640]{1,0:T(8,128)(2,1)S(1)}, bf16[320,640]{1,0:T(8,128)(2,1)S(1)}, u32[]{:S(2)}, u32[]{:S(2)}) collective-permute-start(bf16[320,640]{1,0:T(8,128)(2,1)S(1)} %get-tuple-element.75.refs_6_), channel_id=1, source_target_pairs={{0,8},{4,12},{8,0},{12,4},{16,24},{20,28},{24,16},{28,20},{1,9},{5... | collective-permute-start | bytes 1228808 | tf_op jit(solution)/shard_map/ppermute | solution.py:517
  23.4 11.9 %collective-permute-start.1 = (bf16[2,336,512]{2,1,0:T(8,128)(2,1)S(1)}, bf16[2,336,512]{2,1,0:T(8,128)(2,1)S(1)}, u32[]{:S(2)}, u32[]{:S(2)}) collective-permute-start(bf16[2,336,512]{2,1,0:T(8,128)(2,1)S(1)} %get-tuple-element.77.refs_3_), channel_id=1, source_target_pairs={{0,1},{1,0},{2,3},{3,2},{4,5},{5,4},{6,7},{7,6},{8,9},{9,8},{10,11... | collective-permute-start | bytes 2064392 | tf_op jit(solution)/shard_map/ppermute | solution.py:517
  24.7 16.1 %collective-permute-start.3 = (bf16[256,640]{1,0:T(8,128)(2,1)S(1)}, bf16[256,640]{1,0:T(8,128)(2,1)S(1)}, u32[]{:S(2)}, u32[]{:S(2)}) collective-permute-start(bf16[256,640]{1,0:T(8,128)(2,1)S(1)} %get-tuple-element.85.refs_6_), channel_id=1, source_target_pairs={{0,8},{4,12},{8,0},{12,4},{16,24},{20,28},{24,16},{28,20},{1,9},{5... | collective-permute-start | bytes 983048 | tf_op jit(solution)/shard_map/ppermute | solution.py:517
  25.3 15.6 %collective-permute-start.4 = (bf16[384,640]{1,0:T(8,128)(2,1)S(1)}, bf16[384,640]{1,0:T(8,128)(2,1)S(1)}, u32[]{:S(2)}, u32[]{:S(2)}) collective-permute-start(bf16[384,640]{1,0:T(8,128)(2,1)S(1)} %get-tuple-element.87), channel_id=1, source_target_pairs={{0,4},{4,0},{8,12},{12,8},{16,20},{20,16},{24,28},{28,24},{1,5},{5... | collective-permute-start | bytes 1474568 | tf_op jit(solution)/shard_map/ppermute | solution.py:517
  32.0 12.8 %collective-permute-start.8 = (bf16[160,640]{1,0:T(8,128)(2,1)S(1)}, bf16[160,640]{1,0:T(8,128)(2,1)S(1)}, u32[]{:S(2)}, u32[]{:S(2)}) collective-permute-start(bf16[160,640]{1,0:T(8,128)(2,1)S(1)} %get-tuple-element.96), channel_id=1, source_target_pairs={{0,4},{4,0},{8,12},{12,8},{16,20},{20,16},{24,28},{28,24},{1,5},{5... | collective-permute-start | bytes 614408 | tf_op jit(solution)/shard_map/ppermute | solution.py:517
  32.7 12.2 %collective-permute-start.9 = (bf16[160,640]{1,0:T(8,128)(2,1)S(1)}, bf16[160,640]{1,0:T(8,128)(2,1)S(1)}, u32[]{:S(2)}, u32[]{:S(2)}) collective-permute-start(bf16[160,640]{1,0:T(8,128)(2,1)S(1)} %get-tuple-element.98), channel_id=1, source_target_pairs={{0,16},{4,20},{8,24},{12,28},{16,0},{20,4},{24,8},{28,12},{1,17},{... | collective-permute-start | bytes 614408 | tf_op jit(solution)/shard_map/ppermute | solution.py:517
  35.4 7.5 %collective-permute-start.2 = (bf16[1,336,512]{2,1,0:T(8,128)(2,1)S(1)}, bf16[1,336,512]{2,1,0:T(8,128)(2,1)S(1)}, u32[]{:S(2)}, u32[]{:S(2)}) collective-permute-start(bf16[1,336,512]{2,1,0:T(8,128)(2,1)S(1)} %get-tuple-element.79), channel_id=1, source_target_pairs={{0,2},{1,3},{2,0},{3,1},{4,6},{5,7},{6,4},{7,5},{8,10},{9,11},{10,... | collective-permute-start | bytes 1032200 | tf_op jit(solution)/shard_map/ppermute | solution.py:517
  41.0 8.7 %collective-permute-start.12 = (bf16[128,640]{1,0:T(8,128)(2,1)S(1)}, bf16[128,640]{1,0:T(8,128)(2,1)S(1)}, u32[]{:S(2)}, u32[]{:S(2)}) collective-permute-start(bf16[128,640]{1,0:T(8,128)(2,1)S(1)} %get-tuple-element.104), channel_id=1, source_target_pairs={{0,4},{4,0},{8,12},{12,8},{16,20},{20,16},{24,28},{28,24},{1,5},{5... | collective-permute-start | bytes 491528 | tf_op jit(solution)/shard_map/ppermute | solution.py:517
  41.4 9.9 %collective-permute-start.13 = (bf16[192,640]{1,0:T(8,128)(2,1)S(1)}, bf16[192,640]{1,0:T(8,128)(2,1)S(1)}, u32[]{:S(2)}, u32[]{:S(2)}) collective-permute-start(bf16[192,640]{1,0:T(8,128)(2,1)S(1)} %get-tuple-element.106), channel_id=1, source_target_pairs={{0,8},{4,12},{8,0},{12,4},{16,24},{20,28},{24,16},{28,20},{1,9},{5... | collective-permute-start | bytes 737288 | tf_op jit(solution)/shard_map/ppermute | solution.py:517
  43.4 5.8 %collective-permute-start.15 = (f32[8,384]{1,0:T(8,128)S(1)}, f32[8,384]{1,0:T(8,128)S(1)}, u32[]{:S(2)}, u32[]{:S(2)}) collective-permute-start(f32[8,384]{1,0:T(8,128)S(1)} %get-tuple-element.110.refs_0_), channel_id=1, source_target_pairs={{0,4},{4,0},{8,12},{12,8},{16,20},{20,16},{24,28},{28,24},{1,5},{5... | collective-permute-start | bytes 36872 | tf_op jit(solution)/shard_map/ppermute | solution.py:517
  44.9 15.4 %collective-permute-start.10 = (bf16[80,640]{1,0:T(8,128)(2,1)S(1)}, bf16[80,640]{1,0:T(8,128)(2,1)S(1)}, u32[]{:S(2)}, u32[]{:S(2)}) collective-permute-start(bf16[80,640]{1,0:T(8,128)(2,1)S(1)} %get-tuple-element.100), channel_id=1, source_target_pairs={{0,16},{4,20},{8,24},{12,28},{16,0},{20,4},{24,8},{28,12},{1,17},{... | collective-permute-start | bytes 307208 | tf_op jit(solution)/shard_map/ppermute | solution.py:517
  47.6 12.7 %collective-permute-start.11 = (bf16[80,640]{1,0:T(8,128)(2,1)S(1)}, bf16[80,640]{1,0:T(8,128)(2,1)S(1)}, u32[]{:S(2)}, u32[]{:S(2)}) collective-permute-start(bf16[80,640]{1,0:T(8,128)(2,1)S(1)} %get-tuple-element.102), channel_id=1, source_target_pairs={{0,8},{4,12},{8,0},{12,4},{16,24},{20,28},{24,16},{28,20},{1,9},{5... | collective-permute-start | bytes 307208 | tf_op jit(solution)/shard_map/ppermute | solution.py:517
  49.2 5.2 %collective-permute-start.16 = (f32[8,384]{1,0:T(8,128)S(1)}, f32[8,384]{1,0:T(8,128)S(1)}, u32[]{:S(2)}, u32[]{:S(2)}) collective-permute-start(f32[8,384]{1,0:T(8,128)S(1)} %shard_map.108.refs_0_), channel_id=1, source_target_pairs={{0,8},{4,12},{8,0},{12,4},{16,24},{20,28},{24,16},{28,20},{1,9},{5... | collective-permute-start | bytes 36872 | tf_op jit(solution)/shard_map/ppermute | solution.py:517
  51.5 12.6 %collective-permute-start.14 = (bf16[160,640]{1,0:T(8,128)(2,1)S(1)}, bf16[160,640]{1,0:T(8,128)(2,1)S(1)}, u32[]{:S(2)}, u32[]{:S(2)}) collective-permute-start(bf16[160,640]{1,0:T(8,128)(2,1)S(1)} %get-tuple-element.108), channel_id=1, source_target_pairs={{0,16},{4,20},{8,24},{12,28},{16,0},{20,4},{24,8},{28,12},{1,17},{... | collective-permute-start | bytes 614408 | tf_op jit(solution)/shard_map/ppermute | solution.py:517
  53.1 8.0 %collective-permute-start.7 = (bf16[320,128]{1,0:T(8,128)(2,1)S(1)}, bf16[320,128]{1,0:T(8,128)(2,1)S(1)}, u32[]{:S(2)}, u32[]{:S(2)}) collective-permute-start(bf16[320,128]{1,0:T(8,128)(2,1)S(1)} %get-tuple-element.94), channel_id=1, source_target_pairs={{4,0},{8,4},{12,8},{16,12},{20,16},{24,20},{28,24},{5,1},{9,5},{13... | collective-permute-start | bytes 245768 | tf_op jit(solution)/shard_map/ppermute | solution.py:522
  54.4 9.6 %collective-permute-start.17 = (f32[8,384]{1,0:T(8,128)S(1)}, f32[8,384]{1,0:T(8,128)S(1)}, u32[]{:S(2)}, u32[]{:S(2)}) collective-permute-start(f32[8,384]{1,0:T(8,128)S(1)} %shard_map.109.refs_0_), channel_id=1, source_target_pairs={{0,16},{4,20},{8,24},{12,28},{16,0},{20,4},{24,8},{28,12},{1,17},{... | collective-permute-start | bytes 36872 | tf_op jit(solution)/shard_map/ppermute | solution.py:517
  64.1 1.0 %copy-start.3 = (f32[320]{0:T(512)}, f32[320]{0:T(512)S(1)}, u32[]{:S(2)}) copy-start(f32[320]{0:T(512)S(1)} %slice_reduce_fusion.refs_4_) | copy-start | bytes 3844
